TPU v7x, 128 devices: a whole 4x4x4 slice. The times are simulated.
128 devices in a mesh: rep: 8 (over x, y_lo), shard: 16 (over y_hi, z, core).
Axes of the slice: x: 4, y: 4 (y_hi: 2, y_lo: 2; y = y_hi * 2 + y_lo), z: 4, core: 2. Of those that a mesh axis runs over, the one named last changes fastest.
Arguments:
- tokens: bfloat16 [2, 8192, 1536], P(None, ('rep', 'shard')), may hold values from -6 to 6
- query_weight: bfloat16 [1536, 1536], P('shard'), may hold values from -0.15625 to 0.15625
- key_weight: bfloat16 [1536, 768], P('shard'), may hold values from -0.15625 to 0.15625
- value_weight: bfloat16 [1536, 768], P('shard'), may hold values from -0.15625 to 0.15625
- out_weight: bfloat16 [1536, 1536], P('shard'), may hold values from -0.4375 to 0.4375
- gate_weight: bfloat16 [1536, 4096], P('shard'), may hold values from -0.15625 to 0.15625
- up_weight: bfloat16 [1536, 4096], P('shard'), may hold values from -0.15625 to 0.15625
- down_weight: bfloat16 [4096, 1536], P('shard'), may hold values from -0.09375 to 0.09375
- attention_gain: bfloat16 [1536], P('shard'), may hold values from 0.5 to 1.5
- feedforward_gain: bfloat16 [1536], P('shard'), may hold values from 0.5 to 1.5
- lengths: int32 [2, 8, 32], P(None, 'rep'), may hold values from 19 to 43, as said below
- deal: int32 [2, 8, 32], P(None, 'rep'), may hold values from 0 to 31, as said below
- block_cotangent: bfloat16 [2, 8192, 1536], P(None, ('rep', 'shard')), may hold values from -6 to 6
Outputs:
- block_out: bfloat16 [2, 8192, 1536], P(None, ('rep', 'shard'))
- input_grad: bfloat16 [2, 8192, 1536], P(None, ('rep', 'shard'))
- grad_query: float32 [1536, 1536], P('shard')
- grad_key: float32 [1536, 768], P('shard')
- grad_value: float32 [1536, 768], P('shard')
- grad_output: float32 [1536, 1536], P('shard')
- grad_gate: float32 [1536, 4096], P('shard')
- grad_up: float32 [1536, 4096], P('shard')
- grad_down: float32 [4096, 1536], P('shard')
- grad_attention_gain: float32 [1536], P('shard')
- grad_feedforward_gain: float32 [1536], P('shard')
Inputs may be any that keep to these rules, and one draw needn't show every extreme that they name: `lengths`: for each micro-batch and replica group, the 2 sequences that deal places into one bin have between (585) // 10 and 64 tokens together, and some bin of the group has exactly 64. `deal`: for each micro-batch and replica group, a permutation of the group's 32 sequence numbers; entry b * 2 + s names the sequence in place s of bin b.
All inputs are finite; a program needn't handle non-finite values.
Results may differ from a plain program's by a relative error of at most 0.023.
Values may be sent and summed in bfloat16 or wider, within the bound.
A program may use at most 320 MiB of HBM per device.

v0:
```python
import math

import jax
import jax.numpy as jnp
from jax import lax
from jax.sharding import PartitionSpec as P

D = 1536
QUERY_HEADS = 16
KEY_VALUE_HEADS = 8
HEAD_WIDTH = 96
BIN = 64
MB = 2
SEQ_BIN = 2


eps_norm = 1e-05
rope_base = 100000.0


def sequence_tables(seq_lengths, seq_deal):
    count = seq_lengths.shape[0]
    seq_ids = jnp.arange(count, dtype=jnp.int32)
    seq_start = jnp.cumsum(seq_lengths) - seq_lengths
    matched = seq_deal[:, None] == seq_ids[None, :]
    slot_length = jnp.sum(jnp.where(matched, seq_lengths[None, :], 0), axis=1)
    slot_source = jnp.sum(jnp.where(matched, seq_start[None, :], 0), axis=1)
    slot_of_seq = jnp.sum(jnp.where(matched, seq_ids[:, None], 0), axis=0)
    per_bin = slot_length.reshape(-1, SEQ_BIN)
    slot_begin = (jnp.cumsum(per_bin, axis=1) - per_bin).reshape(-1)
    return (seq_start, slot_length, slot_source, slot_of_seq, slot_begin)


def bin_layout(tables, bin_index, token_rows):
    seq_start, slot_length, slot_source, slot_of_seq, slot_begin = tables
    first = bin_index * SEQ_BIN
    lengths_here = lax.dynamic_slice_in_dim(slot_length, first, SEQ_BIN)
    begins_here = lax.dynamic_slice_in_dim(slot_begin, first, SEQ_BIN)
    sources_here = lax.dynamic_slice_in_dim(slot_source, first, SEQ_BIN)
    row_ids = jnp.arange(token_rows, dtype=jnp.int32)
    ends_here = begins_here + lengths_here
    segment = jnp.sum((row_ids[:, None] >= ends_here[None, :]).astype(jnp.int32), axis=1)
    onehot = segment[:, None] == jnp.arange(SEQ_BIN, dtype=jnp.int32)[None, :]
    token_position = row_ids - jnp.sum(jnp.where(onehot, begins_here[None, :], 0), axis=1)
    source = jnp.sum(jnp.where(onehot, sources_here[None, :], 0), axis=1) + token_position
    return (source, segment < SEQ_BIN, segment, token_position)


def order_layout(tables, seq_lengths, row_ids, token_rows):
    seq_start, slot_length, slot_source, slot_of_seq, slot_begin = tables
    count = seq_lengths.shape[0]
    seq_end = seq_start + seq_lengths
    which = jnp.sum((row_ids[:, None] >= seq_end[None, :]).astype(jnp.int32), axis=1)
    onehot = which[:, None] == jnp.arange(count, dtype=jnp.int32)[None, :]
    inner = row_ids - jnp.sum(jnp.where(onehot, seq_start[None, :], 0), axis=1)
    slot = jnp.sum(jnp.where(onehot, slot_of_seq[None, :], 0), axis=1)
    slot_hot = slot[:, None] == jnp.arange(count, dtype=jnp.int32)[None, :]
    begin = jnp.sum(jnp.where(slot_hot, slot_begin[None, :], 0), axis=1)
    target = slot // SEQ_BIN * token_rows + begin + inner
    return (target, which < count)


def rope_tables(token_position, width):
    half = width // 2
    freq = jnp.exp(jnp.arange(half, dtype=jnp.float32) * (-2.0 * math.log(rope_base) / width))
    angle = token_position.astype(jnp.float32)[:, None] * freq[None, :]
    return (jnp.cos(angle)[:, None, :], jnp.sin(angle)[:, None, :])


def rotary_apply(value_rows, cosine_table, sine_table):
    half = value_rows.shape[-1] // 2
    first = value_rows[..., :half]
    second = value_rows[..., half:]
    return jnp.concatenate(
        [first * cosine_table - second * sine_table, second * cosine_table + first * sine_table],
        axis=-1,
    )


def rotary_inverse(value_rows, cosine_table, sine_table):
    half = value_rows.shape[-1] // 2
    first = value_rows[..., :half]
    second = value_rows[..., half:]
    return jnp.concatenate(
        [first * cosine_table + second * sine_table, second * cosine_table - first * sine_table],
        axis=-1,
    )


def norm_back(grad_normed, normed, inverse, gain):
    scaled = grad_normed * gain
    return inverse * (scaled - normed * jnp.mean(scaled * normed, axis=-1, keepdims=True))


def layer_pass(rows_in, grad_rows, segment, token_position, layer):
    (
        query_full,
        key_full,
        value_full,
        out_full,
        gate_full,
        up_full,
        down_full,
        gain_first,
        gain_second,
    ) = layer
    token_rows = rows_in.shape[0]
    query_per_key = QUERY_HEADS // KEY_VALUE_HEADS
    scale = HEAD_WIDTH ** (-0.5)
    attention_gain = gain_first.astype(jnp.float32)
    feedforward_gain = gain_second.astype(jnp.float32)
    inputs = rows_in.astype(jnp.float32)
    inverse1 = lax.rsqrt(jnp.mean(inputs * inputs, axis=-1, keepdims=True) + eps_norm)
    normal1 = inputs * inverse1
    normed1 = (normal1 * attention_gain).astype(jnp.bfloat16)
    query_projection = jnp.dot(normed1, query_full, preferred_element_type=jnp.float32)
    key_projection = jnp.dot(normed1, key_full, preferred_element_type=jnp.float32)
    value_projection = jnp.dot(normed1, value_full, preferred_element_type=jnp.float32)
    cosine_table, sine_table = rope_tables(token_position, HEAD_WIDTH)
    query_rows = (
        rotary_apply(
            query_projection.reshape(token_rows, QUERY_HEADS, HEAD_WIDTH), cosine_table, sine_table
        )
        .astype(jnp.bfloat16)
        .reshape(token_rows, KEY_VALUE_HEADS, query_per_key, HEAD_WIDTH)
    )
    rotated_keys = rotary_apply(
        key_projection.reshape(token_rows, KEY_VALUE_HEADS, HEAD_WIDTH), cosine_table, sine_table
    ).astype(jnp.bfloat16)
    value_rows = value_projection.astype(jnp.bfloat16).reshape(
        token_rows, KEY_VALUE_HEADS, HEAD_WIDTH
    )
    row_ids = jnp.arange(token_rows, dtype=jnp.int32)
    allowed = (segment[:, None] == segment[None, :]) & (row_ids[None, :] <= row_ids[:, None])
    scores = (
        jnp.einsum("ihgd,jhd->hgij", query_rows, rotated_keys, preferred_element_type=jnp.float32)
        * scale
    )
    scores = jnp.where(allowed, scores, -1e30)
    peak = jnp.max(scores, axis=-1, keepdims=True)
    expo = jnp.exp(scores - peak)
    total = jnp.sum(expo, axis=-1, keepdims=True)
    logsum = peak + jnp.log(total)
    probs_low = (expo / total).astype(jnp.bfloat16)
    mixed = (
        jnp.einsum("hgij,jhd->ihgd", probs_low, value_rows, preferred_element_type=jnp.float32)
        .reshape(token_rows, QUERY_HEADS * HEAD_WIDTH)
        .astype(jnp.bfloat16)
    )
    resid = inputs + jnp.dot(mixed, out_full, preferred_element_type=jnp.float32)
    inverse2 = lax.rsqrt(jnp.mean(resid * resid, axis=-1, keepdims=True) + eps_norm)
    normal2 = resid * inverse2
    normed2 = (normal2 * feedforward_gain).astype(jnp.bfloat16)
    gate = jnp.dot(normed2, gate_full, preferred_element_type=jnp.float32)
    upper = jnp.dot(normed2, up_full, preferred_element_type=jnp.float32)
    sigmoid = jax.nn.sigmoid(gate)
    swish = gate * sigmoid
    hidden = (swish * upper).astype(jnp.bfloat16)
    block_rows = (resid + jnp.dot(hidden, down_full, preferred_element_type=jnp.float32)).astype(
        jnp.bfloat16
    )
    grad_down = jnp.einsum("ik,id->kd", hidden, grad_rows, preferred_element_type=jnp.float32)
    grad_hidden = jnp.einsum("id,kd->ik", grad_rows, down_full, preferred_element_type=jnp.float32)
    grad_gate_in = (grad_hidden * upper * sigmoid * (1.0 + gate * (1.0 - sigmoid))).astype(
        jnp.bfloat16
    )
    grad_up_in = (grad_hidden * swish).astype(jnp.bfloat16)
    grad_gate = jnp.einsum("id,ik->dk", normed2, grad_gate_in, preferred_element_type=jnp.float32)
    grad_up = jnp.einsum("id,ik->dk", normed2, grad_up_in, preferred_element_type=jnp.float32)
    grad_normed2 = jnp.einsum(
        "ik,dk->id", grad_gate_in, gate_full, preferred_element_type=jnp.float32
    )
    grad_normed2 = grad_normed2 + jnp.einsum(
        "ik,dk->id", grad_up_in, up_full, preferred_element_type=jnp.float32
    )
    grad_second_gain = jnp.sum(grad_normed2 * normal2, axis=0)
    grad_resid = grad_rows.astype(jnp.float32) + norm_back(
        grad_normed2, normal2, inverse2, feedforward_gain
    )
    grad_attention = grad_resid.astype(jnp.bfloat16)
    grad_out = jnp.einsum("ie,id->ed", mixed, grad_attention, preferred_element_type=jnp.float32)
    mixed_heads_gradient = jnp.einsum(
        "id,ed->ie", grad_attention, out_full, preferred_element_type=jnp.float32
    )
    mixed_heads_gradient = mixed_heads_gradient.astype(jnp.bfloat16).reshape(
        token_rows, KEY_VALUE_HEADS, query_per_key, HEAD_WIDTH
    )
    again = (
        jnp.einsum("ihgd,jhd->hgij", query_rows, rotated_keys, preferred_element_type=jnp.float32)
        * scale
    )
    probs = jnp.exp(jnp.where(allowed, again, -1e30) - logsum)
    grad_probs = jnp.einsum(
        "ihgd,jhd->hgij", mixed_heads_gradient, value_rows, preferred_element_type=jnp.float32
    )
    spread = jnp.sum(probs * grad_probs, axis=-1, keepdims=True)
    grad_scores = (probs * (grad_probs - spread)).astype(jnp.bfloat16)
    grad_queries = (
        jnp.einsum("hgij,jhd->ihgd", grad_scores, rotated_keys, preferred_element_type=jnp.float32)
        * scale
    )
    key_rows_gradient = (
        jnp.einsum("hgij,ihgd->jhd", grad_scores, query_rows, preferred_element_type=jnp.float32)
        * scale
    )
    value_rows_gradient = jnp.einsum(
        "hgij,ihgd->jhd", probs_low, mixed_heads_gradient, preferred_element_type=jnp.float32
    )
    grad_query_proj = (
        rotary_inverse(
            grad_queries.reshape(token_rows, QUERY_HEADS, HEAD_WIDTH), cosine_table, sine_table
        )
        .reshape(token_rows, QUERY_HEADS * HEAD_WIDTH)
        .astype(jnp.bfloat16)
    )
    key_projection_gradient = (
        rotary_inverse(key_rows_gradient, cosine_table, sine_table)
        .reshape(token_rows, KEY_VALUE_HEADS * HEAD_WIDTH)
        .astype(jnp.bfloat16)
    )
    value_projection_gradient = value_rows_gradient.reshape(
        token_rows, KEY_VALUE_HEADS * HEAD_WIDTH
    ).astype(jnp.bfloat16)
    grad_query = jnp.einsum(
        "id,ie->de", normed1, grad_query_proj, preferred_element_type=jnp.float32
    )
    grad_key = jnp.einsum(
        "id,ie->de", normed1, key_projection_gradient, preferred_element_type=jnp.float32
    )
    grad_value = jnp.einsum(
        "id,ie->de", normed1, value_projection_gradient, preferred_element_type=jnp.float32
    )
    grad_normed1 = jnp.einsum(
        "ie,de->id", grad_query_proj, query_full, preferred_element_type=jnp.float32
    )
    grad_normed1 = grad_normed1 + jnp.einsum(
        "ie,de->id", key_projection_gradient, key_full, preferred_element_type=jnp.float32
    )
    grad_normed1 = grad_normed1 + jnp.einsum(
        "ie,de->id", value_projection_gradient, value_full, preferred_element_type=jnp.float32
    )
    grad_first_gain = jnp.sum(grad_normed1 * normal1, axis=0)
    grad_inputs = grad_resid + norm_back(grad_normed1, normal1, inverse1, attention_gain)
    grads = (
        grad_query,
        grad_key,
        grad_value,
        grad_out,
        grad_gate,
        grad_up,
        grad_down,
        grad_first_gain,
        grad_second_gain,
    )
    return (block_rows, grad_inputs.astype(jnp.bfloat16), grads)


def fetch_layer(shards):
    (
        query_part,
        key_part,
        value_part,
        out_part,
        gate_part,
        up_part,
        down_part,
        first_part,
        second_part,
    ) = shards
    return (
        lax.all_gather(query_part, "shard", axis=0, tiled=True),
        lax.all_gather(key_part, "shard", axis=0, tiled=True),
        lax.all_gather(value_part, "shard", axis=0, tiled=True),
        lax.all_gather(out_part, "shard", axis=0, tiled=True),
        lax.all_gather(gate_part, "shard", axis=0, tiled=True),
        lax.all_gather(up_part, "shard", axis=0, tiled=True),
        lax.all_gather(down_part, "shard", axis=0, tiled=True),
        lax.all_gather(first_part, "shard", axis=0, tiled=True),
        lax.all_gather(second_part, "shard", axis=0, tiled=True),
    )


def reduce_shards(grads):
    (
        query_full,
        key_full,
        value_full,
        out_full,
        gate_full,
        up_full,
        down_full,
        first_full,
        second_full,
    ) = grads
    return (
        lax.psum_scatter(
            query_full.astype(jnp.bfloat16), "shard", scatter_dimension=0, tiled=True
        ).astype(jnp.float32),
        lax.psum_scatter(
            key_full.astype(jnp.bfloat16), "shard", scatter_dimension=0, tiled=True
        ).astype(jnp.float32),
        lax.psum_scatter(
            value_full.astype(jnp.bfloat16), "shard", scatter_dimension=0, tiled=True
        ).astype(jnp.float32),
        lax.psum_scatter(
            out_full.astype(jnp.bfloat16), "shard", scatter_dimension=0, tiled=True
        ).astype(jnp.float32),
        lax.psum_scatter(
            gate_full.astype(jnp.bfloat16), "shard", scatter_dimension=0, tiled=True
        ).astype(jnp.float32),
        lax.psum_scatter(
            up_full.astype(jnp.bfloat16), "shard", scatter_dimension=0, tiled=True
        ).astype(jnp.float32),
        lax.psum_scatter(
            down_full.astype(jnp.bfloat16), "shard", scatter_dimension=0, tiled=True
        ).astype(jnp.float32),
        lax.psum_scatter(
            first_full.astype(jnp.bfloat16), "shard", scatter_dimension=0, tiled=True
        ).astype(jnp.float32),
        lax.psum_scatter(
            second_full.astype(jnp.bfloat16), "shard", scatter_dimension=0, tiled=True
        ).astype(jnp.float32),
    )


def add_all(left_terms, right_terms):
    return tuple((left_term + right_term for left_term, right_term in zip(left_terms, right_terms)))


def take_rows(index_rows, valid_rows, carry, pieces):
    count = pieces[0].shape[0]
    inside = valid_rows & (index_rows >= 0) & (index_rows < count)
    index = jnp.clip(index_rows, 0, count - 1)
    first_rows = jnp.where(inside[:, None], pieces[0][index], carry[0])
    second_rows = jnp.where(inside[:, None], pieces[1][index], carry[1])
    return (first_rows, second_rows)


def body(
    tokens,
    query_weight,
    key_weight,
    value_weight,
    out_weight,
    gate_weight,
    up_weight,
    down_weight,
    attention_gain,
    feedforward_gain,
    lengths,
    deal,
    block_cotangent,
):
    my_bin = lax.axis_index("shard")
    shards = (
        query_weight,
        key_weight,
        value_weight,
        out_weight,
        gate_weight,
        up_weight,
        down_weight,
        attention_gain,
        feedforward_gain,
    )
    summed = tuple((jnp.zeros(shard_part.shape, jnp.float32) for shard_part in shards))
    block_list = []
    grad_list = []
    empty = jnp.zeros((BIN, D), jnp.bfloat16)
    for micro in range(MB):
        tables = sequence_tables(lengths[micro, 0], deal[micro, 0])
        source, bin_valid, segment, token_position = bin_layout(tables, my_bin, BIN)
        given_rows = my_bin * BIN + jnp.arange(BIN, dtype=jnp.int32)
        target, order_valid = order_layout(tables, lengths[micro, 0], given_rows, BIN)
        rows_in, grad_rows = take_rows(
            source,
            bin_valid,
            (empty, empty),
            (
                lax.all_gather(tokens[micro], "shard", axis=0, tiled=True),
                lax.all_gather(block_cotangent[micro], "shard", axis=0, tiled=True),
            ),
        )
        layer = fetch_layer(shards)
        block_rows, input_rows, grads = layer_pass(
            rows_in, grad_rows, segment, token_position, layer
        )
        summed = add_all(summed, reduce_shards(grads))
        out_rows, back_rows = take_rows(
            target,
            order_valid,
            (empty, empty),
            (
                lax.all_gather(block_rows, "shard", axis=0, tiled=True),
                lax.all_gather(input_rows, "shard", axis=0, tiled=True),
            ),
        )
        block_list.append(out_rows)
        grad_list.append(back_rows)
    totals = (
        lax.psum(summed[0].astype(jnp.bfloat16), "rep").astype(jnp.float32),
        lax.psum(summed[1].astype(jnp.bfloat16), "rep").astype(jnp.float32),
        lax.psum(summed[2].astype(jnp.bfloat16), "rep").astype(jnp.float32),
        lax.psum(summed[3].astype(jnp.bfloat16), "rep").astype(jnp.float32),
        lax.psum(summed[4].astype(jnp.bfloat16), "rep").astype(jnp.float32),
        lax.psum(summed[5].astype(jnp.bfloat16), "rep").astype(jnp.float32),
        lax.psum(summed[6].astype(jnp.bfloat16), "rep").astype(jnp.float32),
        lax.psum(summed[7].astype(jnp.bfloat16), "rep").astype(jnp.float32),
        lax.psum(summed[8].astype(jnp.bfloat16), "rep").astype(jnp.float32),
    )
    return (
        jnp.stack(block_list),
        jnp.stack(grad_list),
        totals[0],
        totals[1],
        totals[2],
        totals[3],
        totals[4],
        totals[5],
        totals[6],
        totals[7],
        totals[8],
    )


def solution(mesh):
    placed = (
        P(None, ("rep", "shard"), None),
        P("shard", None),
        P("shard", None),
        P("shard", None),
        P("shard", None),
        P("shard", None),
        P("shard", None),
        P("shard", None),
        P("shard"),
        P("shard"),
        P(None, "rep", None),
        P(None, "rep", None),
        P(None, ("rep", "shard"), None),
    )
    return jax.shard_map(
        body,
        mesh=mesh,
        in_specs=placed,
        out_specs=(
            P(None, ("rep", "shard"), None),
            P(None, ("rep", "shard"), None),
            P("shard", None),
            P("shard", None),
            P("shard", None),
            P("shard", None),
            P("shard", None),
            P("shard", None),
            P("shard", None),
            P("shard"),
            P("shard"),
        ),
        check_vma=False,
    )
```

profile of v0, /device:TPU:1, one launch (start us, length us, event | category | flops | bytes accessed | tf_op | source)
XLA Modules:
  0.0 2558.9 jit_solution(1505098092763901901)
XLA Ops:
  19.0 36.4 %all-reduce.7 = (bf16[1536]{0:T(1024)(128)(2,1)S(1)}, bf16[1536]{0:T(1024)(128)(2,1)S(1)}) all-reduce(bf16[1536]{0:T(1024)(128)(2,1)S(1)} %dynamic-update-slice, bf16[1536]{0:T(1024)(128)(2,1)S(1)} %dynamic-update-slice.1), channel_id=1, replica_groups=mesh['rep'=8,'shard'=16] {'shard'}, use_global_device_ids=true, to_apply=%add | all-reduce | flops 3072 | bytes 12288
  58.9 7.0 all-gather.42.cloned.1.call-done
  69.4 46.1 %all-gather.20.cloned.1.call-done = bf16[1536,768]{1,0:T(8,128)(2,1)} async-done(((bf16[96,768]{1,0:T(8,128)(2,1)}), bf16[1536,768]{1,0:T(8,128)(2,1)}) %all-gather.20.cloned.1.call-update) | async-done | bytes 2359312 | tf_op jit(solution)/shard_map/all_gather | solution.py:273
  118.7 49.5 %all-gather.44.cloned.1.call-done = bf16[1,1024,1536]{2,1,0:T(8,128)(2,1)} async-done(((bf16[1,64,1536]{2,1,0:T(8,128)(2,1)}), bf16[1,1024,1536]{2,1,0:T(8,128)(2,1)}) %all-gather.44.cloned.1.call-update) | async-done | bytes 3145744 | tf_op jit(solution)/shard_map/all_gather | solution.py:380
  173.0 44.6 %all-gather.22.cloned.1.call-done = bf16[1536,768]{1,0:T(8,128)(2,1)} async-done(((bf16[96,768]{1,0:T(8,128)(2,1)}), bf16[1536,768]{1,0:T(8,128)(2,1)}) %all-gather.22.cloned.1.call-update) | async-done | bytes 2359312 | tf_op jit(solution)/shard_map/all_gather | solution.py:272
  222.4 47.8 %all-gather.46.cloned.1.call-done = bf16[1,1024,1536]{2,1,0:T(8,128)(2,1)} async-done(((bf16[1,64,1536]{2,1,0:T(8,128)(2,1)}), bf16[1,1024,1536]{2,1,0:T(8,128)(2,1)}) %all-gather.46.cloned.1.call-update) | async-done | bytes 3145744 | tf_op jit(solution)/shard_map/all_gather | solution.py:381
  274.1 48.6 %all-gather.48.cloned.1.call-done = bf16[1,1024,1536]{2,1,0:T(8,128)(2,1)} async-done(((bf16[1,64,1536]{2,1,0:T(8,128)(2,1)}), bf16[1,1024,1536]{2,1,0:T(8,128)(2,1)}) %all-gather.48.cloned.1.call-update) | async-done | bytes 3145744 | tf_op jit(solution)/shard_map/all_gather | solution.py:381
  327.1 54.5 %all-gather.24.cloned.1.call-done = bf16[1536,1536]{1,0:T(8,128)(2,1)} async-done(((bf16[96,1536]{1,0:T(8,128)(2,1)}), bf16[1536,1536]{1,0:T(8,128)(2,1)}) %all-gather.24.cloned.1.call-update) | async-done | bytes 4718608 | tf_op jit(solution)/shard_map/all_gather | solution.py:271
  393.9 45.6 %all-gather.26.cloned.1.call-done = bf16[1536,1536]{1,0:T(8,128)(2,1)} async-done(((bf16[96,1536]{1,0:T(8,128)(2,1)}), bf16[1536,1536]{1,0:T(8,128)(2,1)}) %all-gather.26.cloned.1.call-update) | async-done | bytes 4718608 | tf_op jit(solution)/shard_map/all_gather | solution.py:274
  446.6 84.0 %all-gather.30.cloned.1.call-done = bf16[1536,4096]{1,0:T(8,128)(2,1)} async-done(((bf16[96,4096]{1,0:T(8,128)(2,1)}), bf16[1536,4096]{1,0:T(8,128)(2,1)}) %all-gather.30.cloned.1.call-update) | async-done | bytes 12582928 | tf_op jit(solution)/shard_map/all_gather | solution.py:276
  530.6 7.8 fusion.114
  538.4 83.0 %all-gather.28.cloned.1.call-done = bf16[1536,4096]{1,0:T(8,128)(2,1)} async-done(((bf16[96,4096]{1,0:T(8,128)(2,1)}), bf16[1536,4096]{1,0:T(8,128)(2,1)}) %all-gather.28.cloned.1.call-update) | async-done | bytes 12582928 | tf_op jit(solution)/shard_map/all_gather | solution.py:275
  621.5 7.8 fusion.113
  629.3 83.2 %all-gather.32.cloned.1.call-done = bf16[4096,1536]{1,0:T(8,128)(2,1)} async-done(((bf16[256,1536]{1,0:T(8,128)(2,1)}), bf16[4096,1536]{1,0:T(8,128)(2,1)}) %all-gather.32.cloned.1.call-update) | async-done | bytes 12582928 | tf_op jit(solution)/shard_map/all_gather | solution.py:277
  712.5 10.4 multiply_convert_fusion.2
  728.0 9.4 multiply_reduce_fusion.3
  738.4 8.1 fusion.116
  746.5 8.1 fusion.115
  754.6 6.7 multiply_convert_fusion
  761.3 8.8 fusion.119
  770.1 9.4 multiply_reduce_fusion.2
  830.3 6.6 convolution_convert_fusion
  837.9 6.5 convolution_convert_fusion.1
  845.4 6.6 convolution_convert_fusion.2
  853.1 6.6 convolution_convert_fusion.3
  860.7 6.5 convolution_convert_fusion.4
  868.3 6.6 convolution_convert_fusion.5
  875.9 7.8 fusion
  897.4 7.6 fusion.1
  906.2 22.3 reduce-scatter.23.cloned.1.call-done
  930.2 73.6 %reduce-scatter.21.cloned.1.call-done = bf16[96,768]{1,0:T(8,128)(2,1)} async-done(((bf16[1536,768]{1,0:T(8,128)(2,1)}), bf16[96,768]{1,0:T(8,128)(2,1)}) %reduce-scatter.21.cloned.1.call-update) | async-done | bytes 147472 | tf_op jit(solution)/shard_map/reduce_scatter | solution.py:299
  1003.8 75.7 %reduce-scatter.19.cloned.1.call-done = bf16[96,768]{1,0:T(8,128)(2,1)} async-done(((bf16[1536,768]{1,0:T(8,128)(2,1)}), bf16[96,768]{1,0:T(8,128)(2,1)}) %reduce-scatter.19.cloned.1.call-update) | async-done | bytes 147472 | tf_op jit(solution)/shard_map/reduce_scatter | solution.py:299
  1081.2 84.8 %reduce-scatter.29.cloned.1.call-done = bf16[96,1536]{1,0:T(8,128)(2,1)} async-done(((bf16[1536,1536]{1,0:T(8,128)(2,1)}), bf16[96,1536]{1,0:T(8,128)(2,1)}) %reduce-scatter.29.cloned.1.call-update) | async-done | bytes 294928 | tf_op jit(solution)/shard_map/reduce_scatter | solution.py:305
  1166.0 86.2 %reduce-scatter.27.cloned.1.call-done = bf16[96,1536]{1,0:T(8,128)(2,1)} async-done(((bf16[1536,1536]{1,0:T(8,128)(2,1)}), bf16[96,1536]{1,0:T(8,128)(2,1)}) %reduce-scatter.27.cloned.1.call-update) | async-done | bytes 294928 | tf_op jit(solution)/shard_map/reduce_scatter | solution.py:305
  1254.0 83.7 %reduce-scatter.15.cloned.1.call-done = bf16[96,1536]{1,0:T(8,128)(2,1)} async-done(((bf16[1536,1536]{1,0:T(8,128)(2,1)}), bf16[96,1536]{1,0:T(8,128)(2,1)}) %reduce-scatter.15.cloned.1.call-update) | async-done | bytes 294928 | tf_op jit(solution)/shard_map/reduce_scatter | solution.py:296
  1337.7 86.3 %reduce-scatter.17.cloned.1.call-done = bf16[96,1536]{1,0:T(8,128)(2,1)} async-done(((bf16[1536,1536]{1,0:T(8,128)(2,1)}), bf16[96,1536]{1,0:T(8,128)(2,1)}) %reduce-scatter.17.cloned.1.call-update) | async-done | bytes 294928 | tf_op jit(solution)/shard_map/reduce_scatter | solution.py:296
  1425.9 124.1 %reduce-scatter.41.cloned.1.call-done = bf16[256,1536]{1,0:T(8,128)(2,1)} async-done(((bf16[4096,1536]{1,0:T(8,128)(2,1)}), bf16[256,1536]{1,0:T(8,128)(2,1)}) %reduce-scatter.41.cloned.1.call-update) | async-done | bytes 786448 | tf_op jit(solution)/shard_map/reduce_scatter | solution.py:314
  1550.0 125.1 %reduce-scatter.39.cloned.1.call-done = bf16[256,1536]{1,0:T(8,128)(2,1)} async-done(((bf16[4096,1536]{1,0:T(8,128)(2,1)}), bf16[256,1536]{1,0:T(8,128)(2,1)}) %reduce-scatter.39.cloned.1.call-update) | async-done | bytes 786448 | tf_op jit(solution)/shard_map/reduce_scatter | solution.py:314
  1677.5 122.6 %reduce-scatter.37.cloned.1.call-done = bf16[96,4096]{1,0:T(8,128)(2,1)} async-done(((bf16[1536,4096]{1,0:T(8,128)(2,1)}), bf16[96,4096]{1,0:T(8,128)(2,1)}) %reduce-scatter.37.cloned.1.call-update) | async-done | bytes 786448 | tf_op jit(solution)/shard_map/reduce_scatter | solution.py:311
  1800.1 125.1 %reduce-scatter.35.cloned.1.call-done = bf16[96,4096]{1,0:T(8,128)(2,1)} async-done(((bf16[1536,4096]{1,0:T(8,128)(2,1)}), bf16[96,4096]{1,0:T(8,128)(2,1)}) %reduce-scatter.35.cloned.1.call-update) | async-done | bytes 786448 | tf_op jit(solution)/shard_map/reduce_scatter | solution.py:311
  1927.6 122.5 %reduce-scatter.33.cloned.1.call-done = bf16[96,4096]{1,0:T(8,128)(2,1)} async-done(((bf16[1536,4096]{1,0:T(8,128)(2,1)}), bf16[96,4096]{1,0:T(8,128)(2,1)}) %reduce-scatter.33.cloned.1.call-update) | async-done | bytes 786448 | tf_op jit(solution)/shard_map/reduce_scatter | solution.py:308
  2050.1 125.1 %reduce-scatter.31.cloned.1.call-done = bf16[96,4096]{1,0:T(8,128)(2,1)} async-done(((bf16[1536,4096]{1,0:T(8,128)(2,1)}), bf16[96,4096]{1,0:T(8,128)(2,1)}) %reduce-scatter.31.cloned.1.call-update) | async-done | bytes 786448 | tf_op jit(solution)/shard_map/reduce_scatter | solution.py:308
  2178.9 60.7 %all-reduce.6 = (bf16[1536]{0:T(1024)(128)(2,1)S(1)}, bf16[1536]{0:T(1024)(128)(2,1)S(1)}, bf16[1536]{0:T(1024)(128)(2,1)S(1)}, bf16[1536]{0:T(1024)(128)(2,1)S(1)}) all-reduce(bf16[1536]{0:T(1024)(128)(2,1)S(1)} %get-tuple-element.17, ...), channel_id=21, replica_groups=mesh['rep'=8,'shard'=16] {'shard'}, use_global_device_ids=true, to_apply=%region_62.63.clone | all-reduce | flops 6144 | bytes 24576
  2239.7 15.4 all-reduce.8
  2259.4 21.6 all-gather.38.cloned.1.call-done
  2284.1 49.4 %all-gather.36.cloned.1.call-done = bf16[1024,1536]{1,0:T(8,128)(2,1)} async-done(((bf16[64,1536]{1,0:T(8,128)(2,1)}), bf16[1024,1536]{1,0:T(8,128)(2,1)}) %all-gather.36.cloned.1.call-update) | async-done | bytes 3145744 | tf_op jit(solution)/shard_map/all_gather | solution.py:394
  2336.7 49.4 %all-gather.40.cloned.1.call-done = bf16[1024,1536]{1,0:T(8,128)(2,1)} async-done(((bf16[64,1536]{1,0:T(8,128)(2,1)}), bf16[1024,1536]{1,0:T(8,128)(2,1)}) %all-gather.40.cloned.1.call-update) | async-done | bytes 3145744 | tf_op jit(solution)/shard_map/all_gather | solution.py:395
  2391.1 148.6 %all-reduce.12.cloned.1.call-done = (bf16[96,1536]{1,0:T(8,128)(2,1)}, bf16[96,768]{1,0:T(8,128)(2,1)}, bf16[96,768]{1,0:T(8,128)(2,1)}, bf16[96,1536]{1,0:T(8,1...) async-done(((bf16[96,1536]{1,0:T(8,128)(2,1)}, bf16[96,768]{1,0:T(8,128)(2,1)}, bf16[96,768]{1,0:T(8,128)(2,1)}, ...) | async-done | bytes 3244048 | tf_op jit(solution)/shard_map/psum | solution.py:401
  (484 shorter events, 177.6 us)
Async XLA Ops:
  7.2 58.7 %all-gather.42.cloned.1.call-start = ((), (), s32[]{:S(2)}) async-start(), calls=%async_computation.39 | async-start | bytes 3342336 | tf_op jit(solution)/shard_map/all_gather | solution.py:380
  9.1 106.4 %all-gather.20.cloned.1.call-start = ((), (), s32[]{:S(2)}) async-start(), calls=%async_computation.14 | async-start | bytes 2506752 | tf_op jit(solution)/shard_map/all_gather | solution.py:273
  9.8 158.3 %all-gather.44.cloned.1.call-start = ((), (), s32[]{:S(2)}) async-start(), calls=%async_computation.40 | async-start | bytes 3342336 | tf_op jit(solution)/shard_map/all_gather | solution.py:380
  10.6 207.1 %all-gather.22.cloned.1.call-start = ((), (), s32[]{:S(2)}) async-start(), calls=%async_computation.15 | async-start | bytes 2506752 | tf_op jit(solution)/shard_map/all_gather | solution.py:272
  11.2 259.0 %all-gather.46.cloned.1.call-start = ((), (), s32[]{:S(2)}) async-start(), calls=%async_computation.41 | async-start | bytes 3342336 | tf_op jit(solution)/shard_map/all_gather | solution.py:381
  13.0 309.7 %all-gather.48.cloned.1.call-start = ((), (), s32[]{:S(2)}) async-start(), calls=%async_computation.42 | async-start | bytes 3342336 | tf_op jit(solution)/shard_map/all_gather | solution.py:381
  13.6 368.0 %all-gather.24.cloned.1.call-start = ((), (), s32[]{:S(2)}) async-start(), calls=%async_computation.16 | async-start | bytes 5013504 | tf_op jit(solution)/shard_map/all_gather | solution.py:271
  14.3 425.1 %all-gather.26.cloned.1.call-start = ((), (), s32[]{:S(2)}) async-start(), calls=%async_computation.17 | async-start | bytes 5013504 | tf_op jit(solution)/shard_map/all_gather | solution.py:274
  15.1 515.5 %all-gather.30.cloned.1.call-start = ((), (), s32[]{:S(2)}) async-start(), calls=%async_computation.19 | async-start | bytes 13369344 | tf_op jit(solution)/shard_map/all_gather | solution.py:276
  15.8 605.6 %all-gather.28.cloned.1.call-start = ((), (), s32[]{:S(2)}) async-start(), calls=%async_computation.18 | async-start | bytes 13369344 | tf_op jit(solution)/shard_map/all_gather | solution.py:275
  16.4 696.1 %all-gather.32.cloned.1.call-start = ((), (), s32[]{:S(2)}) async-start(), calls=%async_computation.20 | async-start | bytes 13369344 | tf_op jit(solution)/shard_map/all_gather | solution.py:277
  17.2 889.1 %reduce-scatter.25.cloned.1.call-start = ((), (), s32[]{:S(2)}) async-start(), calls=%async_computation.30 | async-start | bytes 2506752 | tf_op jit(solution)/shard_map/reduce_scatter | solution.py:302
  58.9 326.1 %copy-start.64 = (f32[64,48]{1,0:T(8,128)}, f32[64,48]{1,0:T(8,128)S(1)}, u32[]{:S(2)}) copy-start(f32[64,48]{1,0:T(8,128)S(1)} %get-tuple-element.91) | copy-start | bytes 36868
  58.9 326.1 %copy-start.67 = (f32[64,48]{1,0:T(8,128)}, f32[64,48]{1,0:T(8,128)S(1)}, u32[]{:S(2)}) copy-start(f32[64,48]{1,0:T(8,128)S(1)} %get-tuple-element.92) | copy-start | bytes 36868
  69.4 312.2 %copy-start.79 = (f32[64]{0:T(128)}, f32[64]{0:T(128)S(1)}, u32[]{:S(2)}) copy-start(f32[64]{0:T(128)S(1)} %add_rsqrt_fusion.3) | copy-start | bytes 772
  171.6 213.9 %copy-start.76 = (f32[64]{0:T(128)}, f32[64]{0:T(128)S(1)}, u32[]{:S(2)}) copy-start(f32[64]{0:T(128)S(1)} %add_rsqrt_fusion.1) | copy-start | bytes 772
  327.1 64.6 %copy-start.54 = (bf16[64,8,48]{2,0,1:T(8,128)(2,1)}, bf16[64,8,48]{2,0,1:T(8,128)(2,1)S(1)}, u32[]{:S(2)}) copy-start(bf16[64,8,48]{2,0,1:T(8,128)(2,1)S(1)} %get-tuple-element.64) | copy-start | bytes 147460
  327.1 64.6 %copy-start.56 = (bf16[64,8,48]{2,0,1:T(8,128)(2,1)}, bf16[64,8,48]{2,0,1:T(8,128)(2,1)S(1)}, u32[]{:S(2)}) copy-start(bf16[64,8,48]{2,0,1:T(8,128)(2,1)S(1)} %get-tuple-element.65) | copy-start | bytes 147460
  445.8 92.7 %copy-start.98 = (f32[64]{0:T(128)}, f32[64]{0:T(128)S(1)}, u32[]{:S(2)}) copy-start(f32[64]{0:T(128)S(1)} %add_rsqrt_fusion.2) | copy-start | bytes 772
  446.6 174.9 %copy-start.19 = (bf16[64,1536]{1,0:T(8,128)(2,1)}, bf16[64,1536]{1,0:T(8,128)(2,1)S(1)}, u32[]{:S(2)}) copy-start(bf16[64,1536]{1,0:T(8,128)(2,1)S(1)} %multiply_convert_fusion.9) | copy-start | bytes 589828
  784.7 143.8 %reduce-scatter.23.cloned.1.call-start = ((), (), s32[]{:S(2)}) async-start(), calls=%async_computation.29 | async-start | bytes 2506752 | tf_op jit(solution)/shard_map/reduce_scatter | solution.py:302
  796.6 207.2 %reduce-scatter.21.cloned.1.call-start = ((), (), s32[]{:S(2)}) async-start(), calls=%async_computation.28 | async-start | bytes 2506752 | tf_op jit(solution)/shard_map/reduce_scatter | solution.py:299
  804.9 274.6 %reduce-scatter.19.cloned.1.call-start = ((), (), s32[]{:S(2)}) async-start(), calls=%async_computation.27 | async-start | bytes 2506752 | tf_op jit(solution)/shard_map/reduce_scatter | solution.py:299
  811.5 354.5 %reduce-scatter.29.cloned.1.call-start = ((), (), s32[]{:S(2)}) async-start(), calls=%async_computation.32 | async-start | bytes 5013504 | tf_op jit(solution)/shard_map/reduce_scatter | solution.py:305
  815.3 436.9 %reduce-scatter.27.cloned.1.call-start = ((), (), s32[]{:S(2)}) async-start(), calls=%async_computation.31 | async-start | bytes 5013504 | tf_op jit(solution)/shard_map/reduce_scatter | solution.py:305
  819.0 518.7 %reduce-scatter.15.cloned.1.call-start = ((), (), s32[]{:S(2)}) async-start(), calls=%async_computation.25 | async-start | bytes 5013504 | tf_op jit(solution)/shard_map/reduce_scatter | solution.py:296
  824.8 599.2 %reduce-scatter.17.cloned.1.call-start = ((), (), s32[]{:S(2)}) async-start(), calls=%async_computation.26 | async-start | bytes 5013504 | tf_op jit(solution)/shard_map/reduce_scatter | solution.py:296
  830.2 719.8 %reduce-scatter.41.cloned.1.call-start = ((), (), s32[]{:S(2)}) async-start(), calls=%async_computation.38 | async-start | bytes 13369344 | tf_op jit(solution)/shard_map/reduce_scatter | solution.py:314
  836.9 838.2 %reduce-scatter.39.cloned.1.call-start = ((), (), s32[]{:S(2)}) async-start(), calls=%async_computation.37 | async-start | bytes 13369344 | tf_op jit(solution)/shard_map/reduce_scatter | solution.py:314
  844.5 955.6 %reduce-scatter.37.cloned.1.call-start = ((), (), s32[]{:S(2)}) async-start(), calls=%async_computation.36 | async-start | bytes 13369344 | tf_op jit(solution)/shard_map/reduce_scatter | solution.py:311
  852.0 1073.1 %reduce-scatter.35.cloned.1.call-start = ((), (), s32[]{:S(2)}) async-start(), calls=%async_computation.35 | async-start | bytes 13369344 | tf_op jit(solution)/shard_map/reduce_scatter | solution.py:311
  859.7 1190.4 %reduce-scatter.33.cloned.1.call-start = ((), (), s32[]{:S(2)}) async-start(), calls=%async_computation.34 | async-start | bytes 13369344 | tf_op jit(solution)/shard_map/reduce_scatter | solution.py:308
  867.3 1307.9 %reduce-scatter.31.cloned.1.call-start = ((), (), s32[]{:S(2)}) async-start(), calls=%async_computation.33 | async-start | bytes 13369344 | tf_op jit(solution)/shard_map/reduce_scatter | solution.py:308
  874.9 1381.2 %all-gather.34.cloned.1.call-start = ((), (), s32[]{:S(2)}) async-start(), calls=%async_computation.21 | async-start | bytes 3342336 | tf_op jit(solution)/shard_map/all_gather | solution.py:394
  883.8 1397.2 %all-gather.38.cloned.1.call-start = ((), (), s32[]{:S(2)}) async-start(), calls=%async_computation.23 | async-start | bytes 3342336 | tf_op jit(solution)/shard_map/all_gather | solution.py:395
  897.3 1436.2 %all-gather.36.cloned.1.call-start = ((), (), s32[]{:S(2)}) async-start(), calls=%async_computation.22 | async-start | bytes 3342336 | tf_op jit(solution)/shard_map/all_gather | solution.py:394
  905.0 1481.2 %all-gather.40.cloned.1.call-start = ((), (), s32[]{:S(2)}) async-start(), calls=%async_computation.24 | async-start | bytes 3342336 | tf_op jit(solution)/shard_map/all_gather | solution.py:395
  905.9 1633.8 %all-reduce.12.cloned.1.call-start = ((), (), s32[]{:S(2)}) async-start(), calls=%async_computation.43 | async-start | bytes 6488064 | tf_op jit(solution)/shard_map/psum | solution.py:401
  1425.9 751.8 %copy-start.93 = (s32[32]{0:T(128)S(1)}, s32[32]{0:T(128)}, u32[]{:S(2)}) copy-start(s32[32]{0:T(128)} %copy-done.92) | copy-start | bytes 388
  1425.9 751.8 %copy-start.95 = (s32[32]{0:T(128)S(1)}, s32[32]{0:T(128)}, u32[]{:S(2)}) copy-start(s32[32]{0:T(128)} %copy-done.94) | copy-start | bytes 388
  1425.9 752.4 %copy-start.97 = (s32[32]{0:T(128)S(1)}, s32[32]{0:T(128)}, u32[]{:S(2)}) copy-start(s32[32]{0:T(128)} %copy-done.96) | copy-start | bytes 388
  1425.9 752.5 %copy-start.102 = (s32[32]{0:T(128)S(1)}, s32[32]{0:T(128)}, u32[]{:S(2)}) copy-start(s32[32]{0:T(128)} %get-tuple-element.30) | copy-start | bytes 388
  1425.9 752.5 %copy-start.108 = (s32[32]{0:T(128)S(1)}, s32[32]{0:T(128)}, u32[]{:S(2)}) copy-start(s32[32]{0:T(128)} %copy-done.107) | copy-start | bytes 388
  1425.9 752.7 %copy-start.91 = (s32[32]{0:T(128)S(1)}, s32[32]{0:T(128)}, u32[]{:S(2)}) copy-start(s32[32]{0:T(128)} %copy-done.90) | copy-start | bytes 388
  1425.9 752.7 %copy-start.101 = (s32[32]{0:T(128)S(1)}, s32[32]{0:T(128)}, u32[]{:S(2)}) copy-start(s32[32]{0:T(128)} %get-tuple-element.129) | copy-start | bytes 388
  1425.9 752.8 %copy-start.106 = (s32[32]{0:T(128)S(1)}, s32[32]{0:T(128)}, u32[]{:S(2)}) copy-start(s32[32]{0:T(128)} %copy-done.105) | copy-start | bytes 388
  1425.9 752.9 %copy-start.86 = (bf16[1536]{0:T(1024)(128)(2,1)S(1)}, bf16[1536]{0:T(1024)(128)(2,1)}, u32[]{:S(2)}) copy-start(bf16[1536]{0:T(1024)(128)(2,1)} %get-tuple-element.11) | copy-start | bytes 9220
  1425.9 752.9 %copy-start.87 = (bf16[1536]{0:T(1024)(128)(2,1)S(1)}, bf16[1536]{0:T(1024)(128)(2,1)}, u32[]{:S(2)}) copy-start(bf16[1536]{0:T(1024)(128)(2,1)} %get-tuple-element.13) | copy-start | bytes 9220
  (98 other events, 972.0 us)
Sparse Core Ops, SparseCore 0:
  11.1 54.8 all-gather.41
  68.4 46.9 all-gather.19
  118.5 49.5 all-gather.43
  170.5 47.1 all-gather.21
  220.5 49.6 all-gather.45
  273.1 49.5 all-gather.47
  325.2 56.3 all-gather.23
  384.0 55.3 all-gather.25
  442.0 88.5 all-gather.29
  532.9 88.5 all-gather.27
  624.0 88.5 all-gather.31
  784.8 67.6 reduce-scatter.24
  857.1 71.3 reduce-scatter.22
  932.4 71.3 reduce-scatter.20
  1008.2 71.2 reduce-scatter.18
  1083.4 82.4 reduce-scatter.28
  1170.5 81.6 reduce-scatter.26
  1256.1 81.5 reduce-scatter.14
  1342.4 81.6 reduce-scatter.16
  1428.2 121.8 reduce-scatter.40
  1554.3 120.7 reduce-scatter.38
  1679.4 120.6 reduce-scatter.36
  1804.4 120.7 reduce-scatter.34
  1929.3 120.7 reduce-scatter.32
  2054.4 120.7 reduce-scatter.30
  2178.1 50.2 all-gather.33
  2231.3 49.5 all-gather.37
  2284.0 49.5 all-gather.35
  2336.6 49.5 all-gather.39
  2390.3 149.4 all-reduce.11
where the time goes:
time: 2570 us; the launch traced here: 2560 us
  waiting for transfers between devices  2130 us (83%)
  matrix products  209 us (8%)
  blocking collectives  112 us (4%)
  local copies, waits for them, and re-layouts  51.9 us (2%)
  other arithmetic  40.2 us (2%)
    reduce_scatter x2, waiting for transfers between devices, reduce_shards(): lax.psum_scatter(down_full.astype(jnp.bfloat16), 'shard', scatter_dimensi...  249 us
    reduce_scatter x2, waiting for transfers between devices, reduce_shards(): lax.psum_scatter(up_full.astype(jnp.bfloat16), 'shard', scatter_dimension...  248 us
    reduce_scatter x2, waiting for transfers between devices, reduce_shards(): lax.psum_scatter(gate_full.astype(jnp.bfloat16), 'shard', scatter_dimensi...  248 us
    reduce_scatter x2, waiting for transfers between devices, reduce_shards(): lax.psum_scatter(out_full.astype(jnp.bfloat16), 'shard', scatter_dimensio...  171 us
    reduce_scatter x2, waiting for transfers between devices, reduce_shards(): lax.psum_scatter(query_full.astype(jnp.bfloat16), 'shard', scatter_dimens...  170 us
    reduce_scatter x2, waiting for transfers between devices, reduce_shards(): lax.psum_scatter(key_full.astype(jnp.bfloat16), 'shard', scatter_dimensio...  149 us
    psum x1, waiting for transfers between devices, body(): lax.psum(summed[0].astype(jnp.bfloat16), 'rep').astype(jnp.float32)  149 us
    unnamed x2, blocking collectives  97.1 us
  transfers between devices with their start and end apart: 30, of which 28 were waited for; matrix products, arithmetic and copies ran while one was open for 8% of the time, Pallas kernels for 0%

commit v1 on v0

v1 whole, which is shorter than its diff:
```python
import math

import jax
import jax.numpy as jnp
from jax import lax
from jax.sharding import PartitionSpec as P

D = 1536
QUERY_HEADS = 16
KEY_VALUE_HEADS = 8
HEAD_WIDTH = 96
QW = QUERY_HEADS * HEAD_WIDTH
KVW = KEY_VALUE_HEADS * HEAD_WIDTH
FF = 4096
BIN = 64
HALO = 48
WIN = BIN + HALO
MB = 2
SHARDS = 16

eps_norm = 1e-05
rope_base = 100000.0


def window_layout(seq_lengths, first_row):
    count = seq_lengths.shape[0]
    ids = jnp.arange(count, dtype=jnp.int32)
    earlier = ids[None, :] < ids[:, None]
    start = jnp.sum(jnp.where(earlier, seq_lengths[None, :], 0), axis=1)
    end = start + seq_lengths
    rows = first_row + jnp.arange(WIN, dtype=jnp.int32)
    which = jnp.sum((rows[:, None] >= end[None, :]).astype(jnp.int32), axis=1)
    onehot = which[:, None] == ids[None, :]
    begin = jnp.sum(jnp.where(onehot, start[None, :], 0), axis=1)
    inside = which < count
    mine = inside & (begin >= first_row) & (begin < first_row + BIN)
    return which, rows - begin, mine, inside


def rope_tables(position):
    half = HEAD_WIDTH // 2
    freq = jnp.exp(jnp.arange(half, dtype=jnp.float32) * (-2.0 * math.log(rope_base) / HEAD_WIDTH))
    angle = position.astype(jnp.float32)[:, None] * freq[None, :]
    return jnp.cos(angle)[:, None, :], jnp.sin(angle)[:, None, :]


def rotate(value, cos, sin):
    half = value.shape[-1] // 2
    first, second = value[..., :half], value[..., half:]
    return jnp.concatenate([first * cos - second * sin, second * cos + first * sin], axis=-1)


def dot(a, b, dims):
    return lax.dot_general(a, b, (dims, ((), ())), preferred_element_type=jnp.float32)


def nn(a, b):
    return dot(a, b, ((1,), (0,)))


def nt(a, b):
    return dot(a, b, ((1,), (1,)))


def tn(a, b):
    return dot(a, b, ((0,), (0,)))


def attention_forward(q, k, v, allowed):
    scale = HEAD_WIDTH ** (-0.5)
    s = jnp.einsum("mihgd,mjhd->mhgij", q, k, preferred_element_type=jnp.float32) * scale
    s = jnp.where(allowed, s, -1e30)
    peak = jnp.max(s, axis=-1, keepdims=True)
    e = jnp.exp(s - peak)
    p = e / jnp.sum(e, axis=-1, keepdims=True)
    p_low = p.astype(jnp.bfloat16)
    o = jnp.einsum("mhgij,mjhd->mihgd", p_low, v, preferred_element_type=jnp.float32)
    return p, p_low, o.astype(jnp.bfloat16)


def layer_pass(x_low, dy, which, position, layer):
    wq, wk, wv, wo, wg, wu, wd, gain1, gain2 = layer
    rows = x_low.shape[0]
    group = QUERY_HEADS // KEY_VALUE_HEADS
    scale = HEAD_WIDTH ** (-0.5)
    gain1 = gain1.astype(jnp.float32)
    gain2 = gain2.astype(jnp.float32)
    x = x_low.astype(jnp.float32)
    r1 = lax.rsqrt(jnp.mean(x * x, axis=-1, keepdims=True) + eps_norm)
    n1 = x * r1
    a1 = (n1 * gain1).astype(jnp.bfloat16)
    cos, sin = rope_tables(position)
    q = rotate(nn(a1, wq).reshape(rows, QUERY_HEADS, HEAD_WIDTH), cos, sin).astype(jnp.bfloat16)
    k = rotate(nn(a1, wk).reshape(rows, KEY_VALUE_HEADS, HEAD_WIDTH), cos, sin).astype(jnp.bfloat16)
    v = nn(a1, wv).astype(jnp.bfloat16)
    q = q.reshape(MB, WIN, KEY_VALUE_HEADS, group, HEAD_WIDTH)
    k = k.reshape(MB, WIN, KEY_VALUE_HEADS, HEAD_WIDTH)
    v = v.reshape(MB, WIN, KEY_VALUE_HEADS, HEAD_WIDTH)
    seg = which.reshape(MB, WIN)
    ids = jnp.arange(WIN, dtype=jnp.int32)
    allowed = (seg[:, :, None] == seg[:, None, :]) & (ids[None, :] <= ids[:, None])[None]
    allowed = allowed[:, None, None]
    p, p_low, o = attention_forward(q, k, v, allowed)
    o = o.reshape(rows, QW)
    x2 = x + nn(o, wo)
    r2 = lax.rsqrt(jnp.mean(x2 * x2, axis=-1, keepdims=True) + eps_norm)
    n2 = x2 * r2
    a2 = (n2 * gain2).astype(jnp.bfloat16)
    g = nn(a2, wg)
    u = nn(a2, wu)
    sig = jax.nn.sigmoid(g)
    sw = g * sig
    hid = (sw * u).astype(jnp.bfloat16)
    block_rows = (x2 + nn(hid, wd)).astype(jnp.bfloat16)

    dhid = nt(dy, wd)
    dg = (dhid * u * sig * (1.0 + g * (1.0 - sig))).astype(jnp.bfloat16)
    du = (dhid * sw).astype(jnp.bfloat16)
    gw_down = tn(hid, dy)
    gw_gate = tn(a2, dg)
    gw_up = tn(a2, du)
    da2 = nt(dg, wg) + nt(du, wu)
    g_gain2 = jnp.sum(da2 * n2, axis=0)
    e2 = da2 * gain2
    dx2 = dy.astype(jnp.float32) + r2 * (e2 - n2 * jnp.mean(e2 * n2, axis=-1, keepdims=True))
    dat = dx2.astype(jnp.bfloat16)
    gw_out = tn(o, dat)
    do = nt(dat, wo).astype(jnp.bfloat16).reshape(MB, WIN, KEY_VALUE_HEADS, group, HEAD_WIDTH)
    dp = jnp.einsum("mihgd,mjhd->mhgij", do, v, preferred_element_type=jnp.float32)
    spread = jnp.sum(p * dp, axis=-1, keepdims=True)
    ds = (p * (dp - spread)).astype(jnp.bfloat16)
    dq = jnp.einsum("mhgij,mjhd->mihgd", ds, k, preferred_element_type=jnp.float32) * scale
    dk = jnp.einsum("mhgij,mihgd->mjhd", ds, q, preferred_element_type=jnp.float32) * scale
    dv = jnp.einsum("mhgij,mihgd->mjhd", p_low, do, preferred_element_type=jnp.float32)
    dqf = rotate(dq.reshape(rows, QUERY_HEADS, HEAD_WIDTH), cos, -sin).reshape(rows, QW).astype(jnp.bfloat16)
    dkf = rotate(dk.reshape(rows, KEY_VALUE_HEADS, HEAD_WIDTH), cos, -sin).reshape(rows, KVW).astype(jnp.bfloat16)
    dvf = dv.reshape(rows, KVW).astype(jnp.bfloat16)
    gw_query = tn(a1, dqf)
    gw_key = tn(a1, dkf)
    gw_value = tn(a1, dvf)
    da1 = nt(dqf, wq) + nt(dkf, wk) + nt(dvf, wv)
    g_gain1 = jnp.sum(da1 * n1, axis=0)
    e1 = da1 * gain1
    dx = dx2 + r1 * (e1 - n1 * jnp.mean(e1 * n1, axis=-1, keepdims=True))
    grads = (gw_query, gw_key, gw_value, gw_out, gw_gate, gw_up, gw_down, g_gain1, g_gain2)
    return block_rows, dx.astype(jnp.bfloat16), grads


def body(
    tokens,
    query_weight,
    key_weight,
    value_weight,
    out_weight,
    gate_weight,
    up_weight,
    down_weight,
    attention_gain,
    feedforward_gain,
    lengths,
    deal,
    block_cotangent,
):
    me = lax.axis_index("shard")
    shards = (
        query_weight,
        key_weight,
        value_weight,
        out_weight,
        gate_weight,
        up_weight,
        down_weight,
        attention_gain,
        feedforward_gain,
    )
    both = jnp.stack([tokens, block_cotangent])
    ahead = [(d, d - 1) for d in range(1, SHARDS)]
    halo = lax.ppermute(both[:, :, :HALO], "shard", ahead)
    window = jnp.concatenate([both, halo], axis=2)
    layout = [window_layout(lengths[m, 0], me * BIN) for m in range(MB)]
    which = jnp.concatenate([one[0] for one in layout])
    position = jnp.concatenate([one[1] for one in layout])
    mine = jnp.concatenate([one[2] for one in layout])
    window = jnp.where(mine[None, :, None], window.reshape(2, MB * WIN, D), 0)
    layer = tuple(lax.all_gather(part, "shard", axis=0, tiled=True) for part in shards)
    position = jnp.where(mine, position, 0)
    block_rows, input_rows, grads = layer_pass(window[0], window[1], which, position, layer)
    results = jnp.stack([block_rows, input_rows]).reshape(2, MB, WIN, D)
    back = [(d, d + 1) for d in range(SHARDS - 1)]
    from_before = lax.ppermute(results[:, :, BIN:], "shard", back)
    from_before = jnp.pad(from_before, ((0, 0), (0, 0), (0, BIN - HALO), (0, 0)))
    mine_own = jnp.stack([one[2][:BIN] for one in layout])[None, :, :, None]
    inside = jnp.stack([one[3][:BIN] for one in layout])[None, :, :, None]
    rows_out = jnp.where(mine_own, results[:, :, :BIN], jnp.where(inside, from_before, 0))
    totals = []
    for part in grads:
        part = lax.psum_scatter(part.astype(jnp.bfloat16), "shard", scatter_dimension=0, tiled=True)
        totals.append(lax.psum(part, "rep").astype(jnp.float32))
    return (rows_out[0], rows_out[1], *totals)


def solution(mesh):
    placed = (
        P(None, ("rep", "shard"), None),
        *([P("shard", None)] * 7),
        P("shard"),
        P("shard"),
        P(None, "rep", None),
        P(None, "rep", None),
        P(None, ("rep", "shard"), None),
    )
    return jax.shard_map(
        body,
        mesh=mesh,
        in_specs=placed,
        out_specs=(
            P(None, ("rep", "shard"), None),
            P(None, ("rep", "shard"), None),
            *([P("shard", None)] * 7),
            P("shard"),
            P("shard"),
        ),
        check_vma=False,
    )
```

time: 2570 us -> 1440 us (0.56)
  waiting for transfers between devices: 2130 us -> 1110 us
  matrix products: 209 us -> 134 us
    reduce_scatter x14 -> x7, waiting for transfers between devices: 1260 us -> 629 us  [body(): lax.psum_scatter(part.astype(jnp.bfloat16), 'shard', scatter_dimension=0,...]
    all_gather x15 -> x7, waiting for transfers between devices: 714 us -> 391 us  [body(): lax.all_gather(part, 'shard', axis=0, tiled=True)]
    dot_general x54 -> x26, matrix products: 209 us -> 132 us  [the longest x21 122 us: dot(): lax.dot_general(a, b, (dims, ((), ())), preferred_element_type=jnp.float32)]
    psum x1, waiting for transfers between devices: 149 us -> 86.7 us  [body(): totals.append(lax.psum(part, 'rep').astype(jnp.float32))]
    gather x8 -> x0, local copies, waits for them, and re-layouts: 26.9 us -> none  [the longest x4 14.1 us: take_rows(): second_rows = jnp.where(inside[:, None], pieces[1][index], carry[1])]
  transfers between devices with their start and end apart: 30 -> 17, of which waited for: 28 -> 15; matrix products, arithmetic and copies ran while one was open for 8% -> 9% of each run, Pallas kernels for 0% -> 0%
where the time goes in v1:
time: 1440 us; the launch traced here: 1430 us
  waiting for transfers between devices  1110 us (77%)
  matrix products  134 us (9%)
  blocking collectives  89 us (6%)
  local copies, waits for them, and re-layouts  50.7 us (4%)
  other arithmetic  23.7 us (2%)
  between operations  16.2 us (1%)
    reduce_scatter x7, waiting for transfers between devices, body(): lax.psum_scatter(part.astype(jnp.bfloat16), 'shard', scatter_dimension=0,...  629 us
    all_gather x7, waiting for transfers between devices, body(): lax.all_gather(part, 'shard', axis=0, tiled=True)  391 us
    dot_general x21, matrix products, dot(): lax.dot_general(a, b, (dims, ((), ())), preferred_element_type=jnp.float32)  122 us
    psum x1, waiting for transfers between devices, body(): totals.append(lax.psum(part, 'rep').astype(jnp.float32))  86.7 us
    unnamed x2, blocking collectives  73.1 us
  transfers between devices with their start and end apart: 17, of which 15 were waited for; matrix products, arithmetic and copies ran while one was open for 9% of the time, Pallas kernels for 0%

profile of v1, /device:TPU:1, one launch (start us, length us, event | category | flops | bytes accessed | tf_op | source)
XLA Modules:
  0.0 1431.9 jit_solution(14137147622246475360)
XLA Ops:
  12.1 3.3 collective-permute-start
  18.8 34.8 %all-reduce.6 = (bf16[1536]{0:T(1024)(128)(2,1)S(1)}, bf16[1536]{0:T(1024)(128)(2,1)S(1)}) all-reduce(bf16[1536]{0:T(1024)(128)(2,1)S(1)} %dynamic-update-slice, bf16[1536]{0:T(1024)(128)(2,1)S(1)} %dynamic-update-slice.1), channel_id=1, replica_groups=mesh['rep'=8,'shard'=16] {'shard'}, use_global_device_ids=true, to_apply=%add.1 | all-reduce | flops 3072 | bytes 12288
  55.3 7.4 all-gather.8.cloned.1.call-done
  62.6 2.4 convolution_convert_fusion.9
  66.6 45.8 %all-gather.10.cloned.1.call-done = bf16[1536,768]{1,0:T(8,128)(2,1)} async-done(((bf16[96,768]{1,0:T(8,128)(2,1)}), bf16[1536,768]{1,0:T(8,128)(2,1)}) %all-gather.10.cloned.1.call-update) | async-done | bytes 2359312 | tf_op jit(solution)/shard_map/all_gather | solution.py:185
  112.4 4.8 copy.77
  117.2 2.5 fusion.36
  120.9 50.5 %all-gather.12.cloned.1.call-done = bf16[1536,1536]{1,0:T(8,128)(2,1)} async-done(((bf16[96,1536]{1,0:T(8,128)(2,1)}), bf16[1536,1536]{1,0:T(8,128)(2,1)}) %all-gather.12.cloned.1.call-update) | async-done | bytes 4718608 | tf_op jit(solution)/shard_map/all_gather | solution.py:185
  171.4 6.6 copy.80
  178.0 3.8 fusion.34
  190.3 38.9 %all-gather.14.cloned.1.call-done = bf16[1536,1536]{1,0:T(8,128)(2,1)} async-done(((bf16[96,1536]{1,0:T(8,128)(2,1)}), bf16[1536,1536]{1,0:T(8,128)(2,1)}) %all-gather.14.cloned.1.call-update) | async-done | bytes 4718608 | tf_op jit(solution)/shard_map/all_gather | solution.py:185
  229.2 3.7 multiply_reduce_fusion.2
  234.5 85.6 %all-gather.18.cloned.1.call-done = bf16[1536,4096]{1,0:T(8,128)(2,1)} async-done(((bf16[96,4096]{1,0:T(8,128)(2,1)}), bf16[1536,4096]{1,0:T(8,128)(2,1)}) %all-gather.18.cloned.1.call-update) | async-done | bytes 12582928 | tf_op jit(solution)/shard_map/all_gather | solution.py:185
  320.1 9.6 fusion.70
  329.7 81.3 %all-gather.16.cloned.1.call-done = bf16[1536,4096]{1,0:T(8,128)(2,1)} async-done(((bf16[96,4096]{1,0:T(8,128)(2,1)}), bf16[1536,4096]{1,0:T(8,128)(2,1)}) %all-gather.16.cloned.1.call-update) | async-done | bytes 12582928 | tf_op jit(solution)/shard_map/all_gather | solution.py:185
  411.0 9.6 fusion.69
  420.7 81.4 %all-gather.20.cloned.1.call-done = bf16[4096,1536]{1,0:T(8,128)(2,1)} async-done(((bf16[256,1536]{1,0:T(8,128)(2,1)}), bf16[4096,1536]{1,0:T(8,128)(2,1)}) %all-gather.20.cloned.1.call-update) | async-done | bytes 12582928 | tf_op jit(solution)/shard_map/all_gather | solution.py:185
  502.0 15.7 %multiply_convert_fusion = (bf16[224,4096]{1,0:T(8,128)(2,1)}, bf16[224,4096]{1,0:T(8,128)(2,1)}, bf16[224,4096]{1,0:T(8,128)(2,1)}) fusion(f32[224,4096]{1,0:T(8,128)} %fusion.69, f32[224,4096]{1,0:T(8,128)} %fusion.70, bf16[4096,1536]{1,0:T(8,128)(2,1)} %all-gather.20.cloned.1.call-done, bf16[2,224,1536]{2,1,0:T(8,128)(2,1)S(1)} %bitcast_select_fusion.2), kind=kOutput, calls=%fused_computation.6 | convolution fusion | flops 2832334848 | bytes 26116096 | tf_op jit(solution)/shard_map/dot_general | solution.py:54
  517.8 10.3 fusion.71
  528.1 9.8 multiply_reduce_fusion
  540.3 2.5 convolution_convert_fusion.7
  542.8 4.5 reshape.350
  547.4 3.6 copy.88
  550.9 2.5 fusion.3
  557.8 2.5 reshape.332
  562.3 2.4 convolution_convert_fusion.6
  564.8 2.8 fusion.27
  571.9 3.3 convolution_convert_fusion.5
  575.2 3.5 convolution_convert_fusion.3
  581.4 2.4 copy.90
  583.7 3.4 reshape.331
  589.8 3.8 convolution_convert_fusion.4
  593.6 8.1 convolution_convert_fusion
  602.8 8.0 convolution_convert_fusion.1
  610.9 7.9 convolution_convert_fusion.2
  620.5 4.2 fusion.72
  628.5 4.2 reduce-scatter.10.cloned.1.call-done
  632.7 76.0 %reduce-scatter.12.cloned.1.call-done = bf16[96,768]{1,0:T(8,128)(2,1)} async-done(((bf16[1536,768]{1,0:T(8,128)(2,1)}), bf16[96,768]{1,0:T(8,128)(2,1)}) %reduce-scatter.12.cloned.1.call-update) | async-done | bytes 147472 | tf_op jit(solution)/shard_map/reduce_scatter | solution.py:197
  708.7 86.5 %reduce-scatter.14.cloned.1.call-done = bf16[96,1536]{1,0:T(8,128)(2,1)} async-done(((bf16[1536,1536]{1,0:T(8,128)(2,1)}), bf16[96,1536]{1,0:T(8,128)(2,1)}) %reduce-scatter.14.cloned.1.call-update) | async-done | bytes 294928 | tf_op jit(solution)/shard_map/reduce_scatter | solution.py:197
  795.2 86.3 %reduce-scatter.8.cloned.1.call-done = bf16[96,1536]{1,0:T(8,128)(2,1)} async-done(((bf16[1536,1536]{1,0:T(8,128)(2,1)}), bf16[96,1536]{1,0:T(8,128)(2,1)}) %reduce-scatter.8.cloned.1.call-update) | async-done | bytes 294928 | tf_op jit(solution)/shard_map/reduce_scatter | solution.py:197
  881.5 126.0 %reduce-scatter.20.cloned.1.call-done = bf16[256,1536]{1,0:T(8,128)(2,1)} async-done(((bf16[4096,1536]{1,0:T(8,128)(2,1)}), bf16[256,1536]{1,0:T(8,128)(2,1)}) %reduce-scatter.20.cloned.1.call-update) | async-done | bytes 786448 | tf_op jit(solution)/shard_map/reduce_scatter | solution.py:197
  1007.4 125.0 %reduce-scatter.18.cloned.1.call-done = bf16[96,4096]{1,0:T(8,128)(2,1)} async-done(((bf16[1536,4096]{1,0:T(8,128)(2,1)}), bf16[96,4096]{1,0:T(8,128)(2,1)}) %reduce-scatter.18.cloned.1.call-update) | async-done | bytes 786448 | tf_op jit(solution)/shard_map/reduce_scatter | solution.py:197
  1132.5 124.9 %reduce-scatter.16.cloned.1.call-done = bf16[96,4096]{1,0:T(8,128)(2,1)} async-done(((bf16[1536,4096]{1,0:T(8,128)(2,1)}), bf16[96,4096]{1,0:T(8,128)(2,1)}) %reduce-scatter.16.cloned.1.call-update) | async-done | bytes 786448 | tf_op jit(solution)/shard_map/reduce_scatter | solution.py:197
  1259.8 7.6 fusion.2
  1267.5 3.5 collective-permute-start.1
  1271.7 38.4 %all-reduce.5 = (bf16[1536]{0:T(1024)(128)(2,1)S(1)}, bf16[1536]{0:T(1024)(128)(2,1)S(1)}) all-reduce(bf16[1536]{0:T(1024)(128)(2,1)S(1)} %get-tuple-element.13, bf16[1536]{0:T(1024)(128)(2,1)S(1)} %copy-done.34), channel_id=9, replica_groups=mesh['rep'=8,'shard'=16] {'shard'}, use_global_device_ids=true, to_apply=%region_28.29.clone | all-reduce | flops 3072 | bytes 12288
  1310.2 15.9 %all-reduce.7 = (bf16[96]{0:T(256)(128)(2,1)S(1)}, bf16[96]{0:T(256)(128)(2,1)S(1)}) all-reduce(bf16[96]{0:T(256)(128)(2,1)S(1)} %dynamic-slice.3, bf16[96]{0:T(256)(128)(2,1)S(1)} %dynamic-slice.5), channel_id=1, replica_groups=mesh['rep'=8,'shard'=16] {'rep'}, use_global_device_ids=true, to_apply=%region_29.30 | all-reduce | flops 192 | bytes 768 | tf_op jit(solution)/shard_map/psum | solution.py:198
  1328.4 86.7 %all-reduce.11.cloned.1.call-done = (bf16[96,1536]{1,0:T(8,128)(2,1)}, bf16[96,768]{1,0:T(8,128)(2,1)}, bf16[96,768]{1,0:T(8,128)(2,1)}, bf16[96,1536]{1,0:T(8,1...) async-done(((bf16[96,1536]{1,0:T(8,128)(2,1)}, bf16[96,768]{1,0:T(8,128)(2,1)}, bf16[96,768]{1,0:T(8,128)(2,1)}, ...) | async-done | bytes 3244048 | tf_op jit(solution)/shard_map/psum | solution.py:198
  (209 shorter events, 61.5 us)
Async XLA Ops:
  7.2 55.4 %all-gather.8.cloned.1.call-start = ((), (), s32[]{:S(2)}) async-start(), calls=%async_computation.7 | async-start | bytes 2506752 | tf_op jit(solution)/shard_map/all_gather | solution.py:185
  7.9 4.1 copy-start.14
  7.9 4.1 copy-start.15
  7.9 104.5 %all-gather.10.cloned.1.call-start = ((), (), s32[]{:S(2)}) async-start(), calls=%async_computation.8 | async-start | bytes 2506752 | tf_op jit(solution)/shard_map/all_gather | solution.py:185
  8.7 162.7 %all-gather.12.cloned.1.call-start = ((), (), s32[]{:S(2)}) async-start(), calls=%async_computation.9 | async-start | bytes 5013504 | tf_op jit(solution)/shard_map/all_gather | solution.py:185
  9.4 219.7 %all-gather.14.cloned.1.call-start = ((), (), s32[]{:S(2)}) async-start(), calls=%async_computation.10 | async-start | bytes 5013504 | tf_op jit(solution)/shard_map/all_gather | solution.py:185
  10.0 310.1 %all-gather.18.cloned.1.call-start = ((), (), s32[]{:S(2)}) async-start(), calls=%async_computation.12 | async-start | bytes 13369344 | tf_op jit(solution)/shard_map/all_gather | solution.py:185
  10.6 4.8 copy-start.33
  10.6 6.4 copy-start.35
  10.6 7.7 copy-start.41
  10.6 8.0 copy-start.42
  10.6 400.4 %all-gather.16.cloned.1.call-start = ((), (), s32[]{:S(2)}) async-start(), calls=%async_computation.11 | async-start | bytes 13369344 | tf_op jit(solution)/shard_map/all_gather | solution.py:185
  11.2 490.8 %all-gather.20.cloned.1.call-start = ((), (), s32[]{:S(2)}) async-start(), calls=%async_computation.13 | async-start | bytes 13369344 | tf_op jit(solution)/shard_map/all_gather | solution.py:185
  11.9 620.7 %reduce-scatter.10.cloned.1.call-start = ((), (), s32[]{:S(2)}) async-start(), calls=%async_computation.15 | async-start | bytes 2506752 | tf_op jit(solution)/shard_map/reduce_scatter | solution.py:197
  12.1 42.6 %collective-permute-start = (bf16[2,2,48,1536]{3,2,1,0:T(8,128)(2,1)S(1)}, bf16[2,2,48,1536]{3,2,1,0:T(8,128)(2,1)S(1)}, u32[]{:S(2)}, u32[]{:S(2)}) collective-permute-start(bf16[2,2,48,1536]{3,2,1,0:T(8,128)(2,1)S(1)} %pad_maximum_fusion.2), channel_id=1, source_target_pairs={{1,0},{2,1},{3,2},{4,3},{5,4},{6,5},{7,6},{8,7},{9,8},{10,9},{11,1... | collective-permute-start | bytes 1769480 | tf_op jit(solution)/shard_map/ppermute | solution.py:178
  16.4 2.2 copy-start.36
  54.6 127.2 %copy-start.17 = (f32[224,48]{0,1:T(8,128)}, f32[224,48]{0,1:T(8,128)S(1)}, u32[]{:S(2)}) copy-start(f32[224,48]{0,1:T(8,128)S(1)} %get-tuple-element.47) | copy-start | bytes 129028
  55.2 122.8 %copy-start.27 = (f32[224]{0:T(256)}, f32[224]{0:T(256)S(1)}, u32[]{:S(2)}) copy-start(f32[224]{0:T(256)S(1)} %add_rsqrt_fusion.1) | copy-start | bytes 2692
  120.0 64.1 %copy-start.19 = (bf16[2,112,8,48]{1,3,2,0:T(8,128)(2,1)}, bf16[2,112,8,48]{1,3,2,0:T(8,128)(2,1)S(1)}, u32[]{:S(2)}) copy-start(bf16[2,112,8,48]{1,3,2,0:T(8,128)(2,1)S(1)} %copy.78) | copy-start | bytes 516100
  186.3 2.7 copy-start.29
  232.8 295.2 %copy-start = (f32[224,1536]{1,0:T(8,128)}, f32[224,1536]{1,0:T(8,128)S(1)}, u32[]{:S(2)}) copy-start(f32[224,1536]{1,0:T(8,128)S(1)} %get-tuple-element.61) | copy-start | bytes 4128772
  517.8 10.3 copy-start.11
  517.8 10.3 copy-start.32
  517.8 22.6 %slice-start = ((s8[4718592]{0:T(1024)(128)(4,1)}), s8[4194304]{0:T(1024)(128)(4,1)S(1)}, s32[]{:S(2)}) async-start(s8[4718592]{0:T(1024)(128)(4,1)} %bitcast.203), calls=%async_computation.22 | async-start | bytes 8388608
  528.0 12.3 slice-start.1
  550.9 2.5 copy-start.13
  550.9 2.5 copy-start.30
  557.8 4.5 copy-start.28
  564.8 143.9 %reduce-scatter.12.cloned.1.call-start = ((), (), s32[]{:S(2)}) async-start(), calls=%async_computation.16 | async-start | bytes 2506752 | tf_op jit(solution)/shard_map/reduce_scatter | solution.py:197
  575.2 220.0 %reduce-scatter.14.cloned.1.call-start = ((), (), s32[]{:S(2)}) async-start(), calls=%async_computation.17 | async-start | bytes 5013504 | tf_op jit(solution)/shard_map/reduce_scatter | solution.py:197
  578.8 302.7 %reduce-scatter.8.cloned.1.call-start = ((), (), s32[]{:S(2)}) async-start(), calls=%async_computation.14 | async-start | bytes 5013504 | tf_op jit(solution)/shard_map/reduce_scatter | solution.py:197
  583.7 3.4 copy-start.18
  583.7 3.4 copy-start.25
  593.6 413.8 %reduce-scatter.20.cloned.1.call-start = ((), (), s32[]{:S(2)}) async-start(), calls=%async_computation.20 | async-start | bytes 13369344 | tf_op jit(solution)/shard_map/reduce_scatter | solution.py:197
  601.7 530.7 %reduce-scatter.18.cloned.1.call-start = ((), (), s32[]{:S(2)}) async-start(), calls=%async_computation.19 | async-start | bytes 13369344 | tf_op jit(solution)/shard_map/reduce_scatter | solution.py:197
  610.8 646.6 %reduce-scatter.16.cloned.1.call-start = ((), (), s32[]{:S(2)}) async-start(), calls=%async_computation.18 | async-start | bytes 13369344 | tf_op jit(solution)/shard_map/reduce_scatter | solution.py:197
  618.8 796.3 %all-reduce.11.cloned.1.call-start = ((), (), s32[]{:S(2)}) async-start(), calls=%async_computation.21 | async-start | bytes 6488064 | tf_op jit(solution)/shard_map/psum | solution.py:198
  620.5 4.2 copy-start.2
  620.5 4.2 copy-start.6
  1257.4 2.3 copy-start.7
  1267.4 3.6 copy-start.43
  1267.4 4.2 copy-start.37
  1267.4 4.3 copy-start.39
  1267.4 4.3 copy-start.34
  1267.5 59.7 %collective-permute-start.1 = (bf16[2,2,48,1536]{3,2,1,0:T(8,128)(2,1)S(1)}, bf16[2,2,48,1536]{3,2,1,0:T(8,128)(2,1)S(1)}, u32[]{:S(2)}, u32[]{:S(2)}) collective-permute-start(bf16[2,2,48,1536]{3,2,1,0:T(8,128)(2,1)S(1)} %pad_maximum_fusion.1), channel_id=1, source_target_pairs={{0,1},{1,2},{2,3},{3,4},{4,5},{5,6},{6,7},{7,8},{8,9},{9,10},{10,1... | collective-permute-start | bytes 1769480 | tf_op jit(solution)/shard_map/ppermute | solution.py:190
  1415.1 5.2 copy-start.26
  1415.1 6.1 copy-start.24
  1420.3 2.2 copy-start.23
  (15 other events, 17.9 us)
Sparse Core Ops, SparseCore 0:
  10.5 52.0 all-gather.7
  65.1 47.2 all-gather.9
  114.9 56.4 all-gather.11
  173.7 55.3 all-gather.13
  231.5 88.5 all-gather.17
  322.5 88.5 all-gather.15
  413.5 88.5 all-gather.19
  564.9 67.7 reduce-scatter.9
  637.2 71.4 reduce-scatter.11
  712.6 82.4 reduce-scatter.13
  799.9 81.5 reduce-scatter.7
  885.6 121.7 reduce-scatter.19
  1011.7 120.6 reduce-scatter.17
  1136.6 120.7 reduce-scatter.15
  1260.3 154.7 all-reduce.10

commit v2 on v1

--- a/solution.py
+++ b/solution.py
@@ -3,6 +3,8 @@
 import jax
 import jax.numpy as jnp
 from jax import lax
+from jax.experimental import pallas as pl
+from jax.experimental.pallas import tpu as pltpu
 from jax.sharding import PartitionSpec as P
 
 D = 1536
@@ -17,9 +19,424 @@
 WIN = BIN + HALO
 MB = 2
 SHARDS = 16
+ROWS = MB * WIN
+MESH = pl.DeviceIdType.MESH
+ANY = pl.BlockSpec(memory_space=pl.ANY)
+DMA = pltpu.SemaphoreType.DMA
 
 eps_norm = 1e-05
 rope_base = 100000.0
+
+
+class Place:
+    def __init__(self):
+        rep, shard = lax.axis_index("rep"), lax.axis_index("shard")
+        self.rep, self.shard = rep, shard
+        self.x, self.yl = rep // 2, rep % 2
+        self.yh, self.z, self.c = shard // 8, (shard // 2) % 4, shard % 2
+        self.y = self.yh * 2 + self.yl
+        self.half = jnp.where(self.yh == self.yl, 1, 0)
+
+    def at(self, x=None, yh=None, yl=None, z=None, c=None):
+        def pick(new, old):
+            return old if new is None else new
+
+        rep = pick(x, self.x) * 2 + pick(yl, self.yl)
+        return rep, pick(yh, self.yh) * 8 + pick(z, self.z) * 2 + pick(c, self.c)
+
+    def along(self, dim):
+        found = []
+        for o in (1, 2, 3):
+            x, yh, yl, z = self.x, self.yh, self.yl, self.z
+            if dim == "x":
+                x = (x + o) % 4
+            elif dim == "z":
+                z = (z + o) % 4
+            else:
+                y = (self.y + o) % 4
+                yh, yl = y // 2, y % 2
+            found.append((x, yh, yl, z))
+        return found
+
+    def peers(self, dim):
+        return [self.at(*where) for where in self.along(dim)]
+
+    def cross(self):
+        return self.at(yh=1 - self.yh, yl=1 - self.yl)
+
+    def inner(self):
+        return self.at(yl=1 - self.yl)
+
+    def sibling(self):
+        return self.at(c=1 - self.c)
+
+    def step(self, by):
+        return self.rep, (self.shard + by + SHARDS) % SHARDS
+
+
+def meet(peers):
+    barrier = pltpu.get_barrier_semaphore()
+    for peer in peers:
+        pl.semaphore_signal(barrier, inc=1, device_id=peer, device_id_type=MESH)
+    pl.semaphore_wait(barrier, len(peers))
+
+
+class Sender:
+    def __init__(self):
+        self.pending = []
+
+    def __call__(self, src, dst, send_sem, recv_sem, to):
+        copy = pltpu.make_async_remote_copy(
+            src_ref=src,
+            dst_ref=dst,
+            send_sem=send_sem,
+            recv_sem=recv_sem,
+            device_id=to,
+            device_id_type=MESH,
+        )
+        copy.start()
+        self.pending.append(copy)
+        return copy
+
+    def drain(self):
+        for copy in self.pending:
+            copy.wait_send()
+
+
+def cut(first, count):
+    if isinstance(first, int):
+        return pl.ds(first, count)
+    return pl.ds(pl.multiple_of(first, 128), count)
+
+
+def rcut(first, count):
+    if isinstance(first, int):
+        return pl.ds(first, count)
+    return pl.ds(pl.multiple_of(first, 16), count)
+
+
+GATE = 4
+QUARTER = FF // 4
+GATHER_UNITS = [(GATE, None, QUARTER), (7, 0, 256), (1, 0, 768), (2, 0, 768), (0, 0, 1536), (3, 0, 1536)]
+GATHER_UNITS += [(5, i * 1024, 1024) for i in range(4)] + [(6, 0, 768), (6, 768, 768)]
+
+
+def gather_kernel(*refs):
+    ins, rows_in, outs, halo = refs[:8], refs[8:10], refs[10:18], refs[18]
+    z_send, z_recv, y_send, y_recv, s_send, s_recv, x_send, x_recv, h_send, h_recv, local_sem = refs[19:]
+    me = Place()
+    meet(me.peers("z") + me.peers("x") + [me.cross(), me.inner(), me.sibling(), me.step(-1), me.step(1)])
+    send = Sender()
+    units = GATHER_UNITS
+    local, z_sent, y_one, y_two, s_sent = {}, {}, {}, {}, []
+
+    def columns(u, half=None):
+        array, first, count = units[u]
+        if first is None:
+            first = me.x * QUARTER
+        if half is None:
+            return cut(first, count)
+        return cut(first + half * (count // 2), count // 2)
+
+    def z_phase(u):
+        a = units[u][0]
+        src, dst = ins[a].at[:, columns(u)], outs[a].at[me.yh, me.z, me.c, :, columns(u)]
+        local[u] = pltpu.make_async_copy(src, dst, local_sem.at[u])
+        local[u].start()
+        z_sent[u] = [send(src, dst, z_send.at[u, i], z_recv.at[u, i], to) for i, to in enumerate(me.peers("z"))]
+
+    def y_phase(u):
+        a = units[u][0]
+        local[u].wait()
+        for copy in z_sent[u]:
+            copy.wait_recv()
+        ref = outs[a].at[me.yh, :, me.c, :, columns(u, me.half)]
+        y_one[u] = send(ref, ref, y_send.at[u, 0], y_recv.at[u, 0], me.cross())
+        if a != GATE:
+            ref = outs[a].at[me.yh, :, me.c, :, columns(u)]
+            s_sent.append(send(ref, ref, s_send.at[u, 0], s_recv.at[u, 0], me.sibling()))
+
+    def forward_phase(u):
+        a = units[u][0]
+        y_one[u].wait_recv()
+        ref = outs[a].at[1 - me.yh, :, me.c, :, columns(u, me.half)]
+        y_two[u] = send(ref, ref, y_send.at[u, 1], y_recv.at[u, 1], me.inner())
+
+    x_sent = []
+
+    def last_phase(u):
+        a = units[u][0]
+        y_two[u].wait_recv()
+        if a == GATE:
+            ref = outs[a].at[:, :, me.c, :, columns(u)]
+            for i, to in enumerate(me.peers("x")):
+                x_sent.append(send(ref, ref, x_send.at[i], x_recv.at[i], to))
+            s_sent.append(send(ref, ref, x_send.at[3], x_recv.at[3], me.sibling()))
+        else:
+            ref = outs[a].at[1 - me.yh, :, me.c, :, columns(u)]
+            s_sent.append(send(ref, ref, s_send.at[u, 1], s_recv.at[u, 1], me.sibling()))
+
+    for i, src in enumerate(rows_in):
+        s_sent.append(send(src.at[:, pl.ds(0, HALO)], halo.at[i], h_send.at[i], h_recv.at[i], me.step(-1)))
+    count = len(units)
+    ahead = 2
+    for u in range(ahead):
+        z_phase(u)
+    for t in range(count + 2):
+        if t + ahead < count:
+            z_phase(t + ahead)
+        if t < count:
+            y_phase(t)
+        if 1 <= t <= count:
+            forward_phase(t - 1)
+        if t >= 2:
+            last_phase(t - 2)
+    for i in range(3):
+        x_sent[i].wait_recv()
+        quarter = (me.x + 3 - i) % 4
+        ref = outs[GATE].at[:, :, me.c, :, cut(quarter * QUARTER, QUARTER)]
+        s_sent.append(send(ref, ref, x_send.at[4 + i], x_recv.at[4 + i], me.sibling()))
+    for copy in s_sent:
+        copy.wait_recv()
+    send.drain()
+
+
+def gather_weights(parts, tokens, cotangent):
+    count = len(GATHER_UNITS)
+    outs = [jax.ShapeDtypeStruct((2, 4, 2, *part.shape), part.dtype) for part in parts]
+    outs.append(jax.ShapeDtypeStruct((2, MB, HALO, D), jnp.bfloat16))
+    results = pl.pallas_call(
+        gather_kernel,
+        out_shape=outs,
+        in_specs=[ANY] * 10,
+        out_specs=[ANY] * 9,
+        scratch_shapes=[DMA((count, 3))] * 2 + [DMA((count, 2))] * 4 + [DMA((7,))] * 2 + [DMA((2,))] * 2 + [DMA((count,))],
+        compiler_params=pltpu.CompilerParams(collective_id=1, has_side_effects=True),
+        name="gather_weights",
+    )(*parts, tokens, cotangent)
+    return [full.reshape(-1, full.shape[-1]) for full in results[:8]], results[8]
+
+
+def exchange_kernel(whole, *refs):
+    count = len(whole)
+    ins, outs = refs[:count], refs[count : 2 * count]
+    send_sem, recv_sem, local_sem = refs[2 * count :]
+    me = Place()
+    meet([me.sibling()])
+    send = Sender()
+    copies = []
+    for i, (src, dst) in enumerate(zip(ins, outs)):
+        width = dst.shape[-1]
+        theirs = src if whole[i] else src.at[:, cut((1 - me.c) * width, width)]
+        own = src if whole[i] else src.at[:, cut(me.c * width, width)]
+        copies.append(send(theirs, dst.at[me.c], send_sem.at[i], recv_sem.at[i], me.sibling()))
+        local = pltpu.make_async_copy(own, dst.at[me.c], local_sem.at[i])
+        local.start()
+        copies.append(local)
+    for copy in copies[1::2]:
+        copy.wait()
+    for copy in copies[::2]:
+        copy.wait_recv()
+    send.drain()
+
+
+def exchange(arrays, whole):
+    count = len(arrays)
+    outs = []
+    for array, full in zip(arrays, whole):
+        rows, width = array.shape
+        outs.append(jax.ShapeDtypeStruct((2, rows, width if full else width // 2), array.dtype))
+    results = pl.pallas_call(
+        lambda *refs: exchange_kernel(whole, *refs),
+        out_shape=outs,
+        in_specs=[ANY] * count,
+        out_specs=[ANY] * count,
+        scratch_shapes=[DMA((count,))] * 3,
+        compiler_params=pltpu.CompilerParams(collective_id=2, has_side_effects=True),
+        name="exchange_rows",
+    )(*arrays)
+    return [both.reshape(-1, both.shape[-1]) for both in results]
+
+
+REDUCE_ROWS = (192, 192, 192, 192, 192, 512, 64)
+REDUCE_COLUMNS = (768, 768, 768, 2048, 2048, 768, 256)
+REDUCE_DIMS = {"A": "zyx", "B": "yxz", "C": "xzy"}
+REDUCE_UNITS = [("A", 3, i * 512, 512) for i in range(4)] + [("A", 0, 0, 768)]
+REDUCE_UNITS += [("B", 4, i * 512, 512) for i in range(4)] + [("B", 1, 0, 768)]
+REDUCE_UNITS += [("C", 5, i * 256, 256) for i in range(3)] + [("C", 2, 0, 768), ("C", 6, 0, 256)]
+ROUNDS = [(t, 5 + t, 10 + t) for t in range(5)]
+GAINS = 6
+
+
+def reduce_shapes(u):
+    order, a, _, n = REDUCE_UNITS[u]
+    r = REDUCE_ROWS[a]
+    first = {"A": (2, r, n), "B": (4, r, n // 2), "C": (2, 4, r // 4, n)}[order]
+    second = {"A": (r, n // 2), "B": (4, r // 4, n // 2), "C": (2, r // 4, n)}[order]
+    return first, second, (r // 4, n // 2)
+
+
+def add_into(total, parts):
+    *lead, rows, _ = total.shape
+    blocks = rows // 16
+
+    def step(i, carry):
+        where, rest = [], i // blocks
+        for n in reversed(lead):
+            where.insert(0, rest % n)
+            rest = rest // n
+        where = (*where, rcut((i % blocks) * 16, 16), slice(None))
+        s = total[where].astype(jnp.float32)
+        for k in range(3):
+            s = s + parts[(k, *where)].astype(jnp.float32)
+        total[where] = s.astype(jnp.bfloat16)
+        return carry
+
+    lax.fori_loop(0, math.prod(lead) * blocks, step, 0)
+
+
+def reduce_kernel(*refs):
+    nu = len(REDUCE_UNITS)
+    ins, rows_in, outs, halo, totals = refs[:7], refs[7:9], refs[9:16], refs[16], refs[17:23]
+    rest = refs[23:]
+    kept = (rest[:nu], rest[nu : 2 * nu], rest[2 * nu : 3 * nu])
+    taken = (rest[3 * nu : 4 * nu], rest[4 * nu : 5 * nu], rest[5 * nu : 6 * nu])
+    send_sem, recv_sem, g_send, g_recv, s_send, s_recv, h_send, h_recv, local_sem, final_sem = rest[6 * nu :]
+    totals = (*totals, outs[GAINS])
+    me = Place()
+    meet(me.peers("z") + me.peers("x") + me.peers("y") + [me.sibling(), me.step(-1), me.step(1)])
+    send = Sender()
+    sent, own = {}, {}
+
+    def share(u, stage, x, yh, yl, z):
+        order, a, first, n = REDUCE_UNITS[u]
+        r = REDUCE_ROWS[a] // 4
+        src = ins[a] if stage == 0 else kept[stage - 1][u]
+        begin = first if stage == 0 else 0
+        dim = REDUCE_DIMS[order][stage]
+        lead = {"A": 2, "B": 2, "C": 2}[order] if stage == 0 else len(src.shape) - 2
+        columns = slice(None) if stage else cut(begin, n)
+        if dim == "z":
+            return src.at[:, z, :, columns] if lead == 2 else src.at[z]
+        if dim == "x":
+            rows = rcut(x * r, r)
+            if lead == 2:
+                return src.at[:, :, rows, columns]
+            return src.at[:, rows] if lead == 1 else src.at[rows]
+        columns = cut(begin + yl * (n // 2), n // 2)
+        if lead == 2:
+            return src.at[yh, :, :, columns]
+        return src.at[yh, :, columns]
+
+    def issue(u, stage):
+        dim = REDUCE_DIMS[REDUCE_UNITS[u][0]][stage]
+        sent[u, stage] = [
+            send(share(u, stage, *where), taken[stage][u].at[i], send_sem.at[u, stage, i], recv_sem.at[u, stage, i], me.at(*where))
+            for i, where in enumerate(me.along(dim))
+        ]
+        own[u, stage] = pltpu.make_async_copy(
+            share(u, stage, me.x, me.yh, me.yl, me.z), kept[stage][u], local_sem.at[u, stage]
+        )
+        own[u, stage].start()
+
+    def finish(u, stage):
+        own[u, stage].wait()
+        for copy in sent[u, stage]:
+            copy.wait_recv()
+        add_into(kept[stage][u], taken[stage][u])
+
+    def result(u, all_x, all_y):
+        order, a, first, n = REDUCE_UNITS[u]
+        r = REDUCE_ROWS[a] // 4
+        rows = slice(None) if all_x else rcut(me.x * r, r)
+        columns = cut(first, n) if all_y else cut(first + me.yl * (n // 2), n // 2)
+        return totals[a].at[rows, columns]
+
+    def spread_one(u):
+        order = REDUCE_UNITS[u][0]
+        dst = result(u, False, False)
+        own[u, 3] = pltpu.make_async_copy(kept[2][u], dst, local_sem.at[u, 3])
+        own[u, 3].start()
+        to = [me.inner()] if order == "C" else me.peers("x")
+        sent[u, 3] = [send(kept[2][u], dst, g_send.at[u, i], g_recv.at[u, i], one) for i, one in enumerate(to)]
+
+    def spread_two(u):
+        order = REDUCE_UNITS[u][0]
+        own[u, 3].wait()
+        for copy in sent[u, 3]:
+            copy.wait_recv()
+        ref = result(u, order != "C", order == "C")
+        to = me.peers("x") if order == "C" else [me.inner()]
+        sent[u, 4] = [send(ref, ref, g_send.at[u, 3 + i], g_recv.at[u, 3 + i], one) for i, one in enumerate(to)]
+
+    last = []
+
+    def deliver(u):
+        order, a, first, n = REDUCE_UNITS[u]
+        for copy in sent[u, 4]:
+            copy.wait_recv()
+        if a == GAINS:
+            return
+        r, width = REDUCE_ROWS[a] // 2, REDUCE_COLUMNS[a]
+        dst = outs[a].at[:, cut(me.c * width + first, n)]
+        last.append(send(totals[a].at[rcut((1 - me.c) * r, r), cut(first, n)], dst, s_send.at[u], s_recv.at[u], me.sibling()))
+        own[u, 5] = pltpu.make_async_copy(totals[a].at[rcut(me.c * r, r), cut(first, n)], dst, final_sem.at[u])
+        own[u, 5].start()
+
+    for i, src in enumerate(rows_in):
+        last.append(send(src.at[:, pl.ds(BIN, HALO)], halo.at[i], h_send.at[i], h_recv.at[i], me.step(1)))
+    count = len(ROUNDS)
+    for u in ROUNDS[0]:
+        issue(u, 0)
+    for t in range(count + 4):
+        if t + 1 < count:
+            for u in ROUNDS[t + 1]:
+                issue(u, 0)
+        for stage in range(2):
+            if 0 <= t - stage < count:
+                for u in ROUNDS[t - stage]:
+                    finish(u, stage)
+                    issue(u, stage + 1)
+        if 0 <= t - 2 < count:
+            for u in ROUNDS[t - 2]:
+                finish(u, 2)
+                spread_one(u)
+        if 0 <= t - 3 < count:
+            for u in ROUNDS[t - 3]:
+                spread_two(u)
+        if 0 <= t - 4 < count:
+            for u in ROUNDS[t - 4]:
+                deliver(u)
+    for u in range(nu):
+        if (u, 5) in own:
+            own[u, 5].wait()
+    for copy in last:
+        copy.wait_recv()
+    send.drain()
+
+
+def reduce_grads(grads, block_rows, input_rows):
+    nu = len(REDUCE_UNITS)
+    first, second, third = zip(*[reduce_shapes(u) for u in range(nu)])
+    low = jnp.bfloat16
+    shapes = list(zip(REDUCE_ROWS, REDUCE_COLUMNS))
+    outs = [jax.ShapeDtypeStruct((r // 2, 2 * n), low) for r, n in shapes[:GAINS]]
+    outs.append(jax.ShapeDtypeStruct(shapes[GAINS], low))
+    outs.append(jax.ShapeDtypeStruct((2, MB, HALO, D), low))
+    outs += [jax.ShapeDtypeStruct(shape, low) for shape in shapes[:GAINS]]
+    scratch = [pltpu.VMEM(s, low) for s in (*first, *second, *third)]
+    scratch += [pltpu.VMEM((3, *s), low) for s in (*first, *second, *third)]
+    scratch += [DMA((nu, 3, 3))] * 2 + [DMA((nu, 6))] * 2 + [DMA((nu,))] * 2 + [DMA((2,))] * 2 + [DMA((nu, 4)), DMA((nu,))]
+    results = pl.pallas_call(
+        reduce_kernel,
+        out_shape=outs,
+        in_specs=[ANY] * 9,
+        out_specs=[ANY] * len(outs),
+        scratch_shapes=scratch,
+        compiler_params=pltpu.CompilerParams(collective_id=3, has_side_effects=True, vmem_limit_bytes=56 * 2**20),
+        name="reduce_grads",
+    )(*grads, block_rows, input_rows)
+    return results[:GAINS], results[GAINS], results[GAINS + 1]
 
 
 def window_layout(seq_lengths, first_row):
@@ -116,15 +533,11 @@
     dhid = nt(dy, wd)
     dg = (dhid * u * sig * (1.0 + g * (1.0 - sig))).astype(jnp.bfloat16)
     du = (dhid * sw).astype(jnp.bfloat16)
-    gw_down = tn(hid, dy)
-    gw_gate = tn(a2, dg)
-    gw_up = tn(a2, du)
     da2 = nt(dg, wg) + nt(du, wu)
     g_gain2 = jnp.sum(da2 * n2, axis=0)
     e2 = da2 * gain2
     dx2 = dy.astype(jnp.float32) + r2 * (e2 - n2 * jnp.mean(e2 * n2, axis=-1, keepdims=True))
     dat = dx2.astype(jnp.bfloat16)
-    gw_out = tn(o, dat)
     do = nt(dat, wo).astype(jnp.bfloat16).reshape(MB, WIN, KEY_VALUE_HEADS, group, HEAD_WIDTH)
     dp = jnp.einsum("mihgd,mjhd->mhgij", do, v, preferred_element_type=jnp.float32)
     spread = jnp.sum(p * dp, axis=-1, keepdims=True)
@@ -135,15 +548,13 @@
     dqf = rotate(dq.reshape(rows, QUERY_HEADS, HEAD_WIDTH), cos, -sin).reshape(rows, QW).astype(jnp.bfloat16)
     dkf = rotate(dk.reshape(rows, KEY_VALUE_HEADS, HEAD_WIDTH), cos, -sin).reshape(rows, KVW).astype(jnp.bfloat16)
     dvf = dv.reshape(rows, KVW).astype(jnp.bfloat16)
-    gw_query = tn(a1, dqf)
-    gw_key = tn(a1, dkf)
-    gw_value = tn(a1, dvf)
     da1 = nt(dqf, wq) + nt(dkf, wk) + nt(dvf, wv)
     g_gain1 = jnp.sum(da1 * n1, axis=0)
     e1 = da1 * gain1
     dx = dx2 + r1 * (e1 - n1 * jnp.mean(e1 * n1, axis=-1, keepdims=True))
-    grads = (gw_query, gw_key, gw_value, gw_out, gw_gate, gw_up, gw_down, g_gain1, g_gain2)
-    return block_rows, dx.astype(jnp.bfloat16), grads
+    lefts = (a1, o, a2, hid)
+    rights = (dqf, jnp.concatenate([dkf, dvf], axis=1), dat, dg, du)
+    return block_rows, dx.astype(jnp.bfloat16), lefts, rights, (g_gain1, g_gain2)
 
 
 def body(
@@ -162,7 +573,10 @@
     block_cotangent,
 ):
     me = lax.axis_index("shard")
-    shards = (
+    core = me % 2
+    gains = jnp.pad(jnp.stack([attention_gain, feedforward_gain]), ((0, 0), (0, 32))).reshape(1, 256)
+    gains = jnp.pad(gains, ((0, 15), (0, 0)))
+    parts = (
         query_weight,
         key_weight,
         value_weight,
@@ -170,33 +584,55 @@
         gate_weight,
         up_weight,
         down_weight,
-        attention_gain,
-        feedforward_gain,
+        gains,
     )
-    both = jnp.stack([tokens, block_cotangent])
-    ahead = [(d, d - 1) for d in range(1, SHARDS)]
-    halo = lax.ppermute(both[:, :, :HALO], "shard", ahead)
-    window = jnp.concatenate([both, halo], axis=2)
+    full, halo = gather_weights(parts, tokens, block_cotangent)
+    gains_full = full[7].reshape(SHARDS, 16, 2, 128)[:, 0, :, :96]
+    layer = (*full[:7], gains_full[:, 0].reshape(D), gains_full[:, 1].reshape(D))
+    window = jnp.concatenate([jnp.stack([tokens, block_cotangent]), halo], axis=2)
     layout = [window_layout(lengths[m, 0], me * BIN) for m in range(MB)]
     which = jnp.concatenate([one[0] for one in layout])
     position = jnp.concatenate([one[1] for one in layout])
     mine = jnp.concatenate([one[2] for one in layout])
-    window = jnp.where(mine[None, :, None], window.reshape(2, MB * WIN, D), 0)
-    layer = tuple(lax.all_gather(part, "shard", axis=0, tiled=True) for part in shards)
+    window = jnp.where(mine[None, :, None], window.reshape(2, ROWS, D), 0)
     position = jnp.where(mine, position, 0)
-    block_rows, input_rows, grads = layer_pass(window[0], window[1], which, position, layer)
-    results = jnp.stack([block_rows, input_rows]).reshape(2, MB, WIN, D)
-    back = [(d, d + 1) for d in range(SHARDS - 1)]
-    from_before = lax.ppermute(results[:, :, BIN:], "shard", back)
+    dy = window[1]
+    block_rows, input_rows, lefts, rights, gain_grads = layer_pass(window[0], dy, which, position, layer)
+
+    gain_rows = jnp.pad(jnp.stack(gain_grads), ((0, 14), (0, 0))).astype(jnp.bfloat16)
+    arrays = (*lefts, gain_rows, *rights, dy)
+    both = exchange(arrays, (True,) * 5 + (False,) * 6)
+    a1, o, a2, hid, gain_both, dqf, dkv, dat, dg, du, dy = both
+    pairs = ((a1, dqf), (a1, dkv), (o, dat), (a2, dg), (a2, du), (hid, dy))
+    grads = [tn(left, right).astype(jnp.bfloat16) for left, right in pairs]
+    grads = [grad.reshape(2, 4, -1, grad.shape[-1]) for grad in grads]
+    gain_both = gain_both.astype(jnp.float32).reshape(2, 16, D)
+    gain_sum = (gain_both[0, :2] + gain_both[1, :2]).reshape(2, 2, 4, 192).transpose(1, 2, 0, 3)
+    gain_sum = jnp.pad(gain_sum, ((0, 0), (0, 0), (0, 62), (0, 64))).astype(jnp.bfloat16)
+    totals, gain_totals, from_before = reduce_grads(
+        (*grads, gain_sum), block_rows.reshape(MB, WIN, D), input_rows.reshape(MB, WIN, D)
+    )
+
+    results = jnp.stack([block_rows, input_rows]).reshape(2, MB, WIN, D)[:, :, :BIN]
     from_before = jnp.pad(from_before, ((0, 0), (0, 0), (0, BIN - HALO), (0, 0)))
     mine_own = jnp.stack([one[2][:BIN] for one in layout])[None, :, :, None]
     inside = jnp.stack([one[3][:BIN] for one in layout])[None, :, :, None]
-    rows_out = jnp.where(mine_own, results[:, :, :BIN], jnp.where(inside, from_before, 0))
-    totals = []
-    for part in grads:
-        part = lax.psum_scatter(part.astype(jnp.bfloat16), "shard", scatter_dimension=0, tiled=True)
-        totals.append(lax.psum(part, "rep").astype(jnp.float32))
-    return (rows_out[0], rows_out[1], *totals)
+    rows_out = jnp.where(mine_own, results, jnp.where(inside, from_before, 0))
+    g_query, g_kv, g_out, g_gate, g_up, g_down = [total.astype(jnp.float32) for total in totals]
+    gain_out = lax.dynamic_slice_in_dim(gain_totals[:2].astype(jnp.float32), core * 96, 96, axis=1)
+    return (
+        rows_out[0],
+        rows_out[1],
+        g_query,
+        g_kv[:, :KVW],
+        g_kv[:, KVW:],
+        g_out,
+        g_gate,
+        g_up,
+        g_down,
+        gain_out[0],
+        gain_out[1],
+    )
 
 
 def solution(mesh):

time: 1440 us -> 793 us (0.55)
  waiting for transfers between devices: 1110 us -> 0 us
  Pallas kernels: 0 us -> 587 us
  blocking collectives: 89 us -> 0 us
  matrix products: 134 us -> 117 us
  between operations: 16.2 us -> 1.75 us
    reduce_scatter x7 -> x0, waiting for transfers between devices: 629 us -> none  [body(): lax.psum_scatter(part.astype(jnp.bfloat16), 'shard', scatter_dimension=0,...]
    pallas_call x0 -> x3, Pallas kernels: none -> 587 us  [the longest x1 218 us: exchange(): pl.pallas_call(lambda *refs: exchange_kernel(whole, *refs), out_shape=out...]
    all_gather x7 -> x0, waiting for transfers between devices: 391 us -> none  [body(): lax.all_gather(part, 'shard', axis=0, tiled=True)]
    psum x1 -> x0, waiting for transfers between devices: 86.7 us -> none  [body(): totals.append(lax.psum(part, 'rep').astype(jnp.float32))]
    unnamed x2 -> x0, blocking collectives: 73.1 us -> none
    psum x1 -> x0, blocking collectives: 15.9 us -> none  [body(): totals.append(lax.psum(part, 'rep').astype(jnp.float32))]
    dot_general x21 -> x20, matrix products: 122 us -> 106 us  [dot(): lax.dot_general(a, b, (dims, ((), ())), preferred_element_type=jnp.float32)]
  transfers between devices with their start and end apart: 17 -> 0, of which waited for: 15 -> 0; matrix products, arithmetic and copies ran while one was open for 9% -> 0% of each run, Pallas kernels for 0% -> 0%
where the time goes in v2:
time: 793 us; the launch traced here: 786 us
  Pallas kernels  587 us (74%)
  matrix products  117 us (15%)
  local copies, waits for them, and re-layouts  54.8 us (7%)
  other arithmetic  25.2 us (3%)
    pallas_call x1, Pallas kernels, exchange(): pl.pallas_call(lambda *refs: exchange_kernel(whole, *refs), out_shape=out...  218 us
    pallas_call x1, Pallas kernels, reduce_grads(): pl.pallas_call(reduce_kernel, out_shape=outs, in_specs=[ANY] * 9, out_spe...  194 us
    pallas_call x1, Pallas kernels, gather_weights(): pl.pallas_call(gather_kernel, out_shape=outs, in_specs=[ANY] * 10, out_sp...  175 us
    dot_general x20, matrix products, dot(): lax.dot_general(a, b, (dims, ((), ())), preferred_element_type=jnp.float32)  106 us

profile of v2, /device:TPU:1, one launch (start us, length us, event | category | flops | bytes accessed | tf_op | source)
XLA Modules:
  0.0 785.8 jit_solution(14754060703898297582)
XLA Ops:
  4.8 174.9 %gather_weights.1 = (bf16[2,4,2,96,1536]{4,3,2,1,0:T(8,128)(2,1)}, bf16[2,4,2,96,768]{4,3,2,1,0:T(8,128)(2,1)}, bf16[2,4,2,96,768]{4,3,2,1,0:T(8,128)(2,1)}, bf1...) custom-call(bf16[96,1536]{1,0:T(8,128)(2,1)} %refs_0_.1, ...), custom_call_target="tpu_custom_call" | custom-call | tf_op jit(solution)/shard_map/gather_weights/pallas_call | solution.py:208
  179.8 1.2 pad_maximum_fusion
  181.2 10.2 %fusion.62 = f32[224,4096]{1,0:T(8,128)} fusion(bf16[4096,1536]{1,0:T(8,128)(2,1)} %bitcast.286, bf16[2,224,1536]{2,1,0:T(8,128)(2,1)S(1)} %bitcast_select_fusion.2), kind=kOutput, calls=%fused_computation.160 | convolution fusion | flops 2818572288 | bytes 16941056 | tf_op jit(solution)/shard_map/dot_general | solution.py:471
  192.4 2.4 convolution_convert_fusion.2
  196.4 4.5 copy.66
  200.9 2.5 fusion.34
  205.5 6.7 copy.69
  212.2 3.8 fusion.32
  218.0 2.1 fusion.68
  220.1 1.2 copy-done.15
  221.3 1.4 fusion.23
  224.0 3.7 multiply_reduce_fusion.2
  229.9 6.8 fusion.69
  236.8 10.4 %multiply_convert_fusion.2 = (bf16[224,4096]{1,0:T(8,128)(2,1)}, bf16[224,4096]{1,0:T(8,128)(2,1)S(1)}, bf16[224,4096]{1,0:T(8,128)(2,1)S(1)}) fusion(f32[224,4096]{1,0:T(8,128)S(1)} %fusion.69, f32[224,4096]{1,0:T(8,128)S(1)} %copy-done.54, bf16[224,1536]{1,0:T(8,128)(2,1)S(1)} %multiply_convert_fusion.3.refs_2_, bf16[1536,4096]{1,0:T(8,128)(2,1)} %bitcast.288), kind=kOutput, calls=%fused_computation.9 | convolution fusion | flops 2832334848 | bytes 26116096 | tf_op jit(solution)/shard_map/dot_general | solution.py:471
  247.1 10.9 %fusion.70 = f32[224,1536]{1,0:T(8,128)} fusion(bf16[224,4096]{1,0:T(8,128)(2,1)S(1)} %get-tuple-element.78.refs_8_, bf16[1536,4096]{1,0:T(8,128)(2,1)} %bitcast.291), kind=kOutput, calls=%fused_computation.165 | convolution fusion | flops 2818572288 | bytes 15794176 | tf_op jit(solution)/shard_map/dot_general | solution.py:471
  258.0 9.8 %multiply_reduce_fusion = (bf16[1536]{0:T(1024)(128)(2,1)}, f32[224]{0:T(256)}, f32[224,1536]{1,0:T(8,128)S(1)}) fusion(f32[224,1536]{1,0:T(8,128)S(1)} %get-tuple-element.110, f32[224]{0:T(256)S(1)} %copy-done.31, f32[1536]{0:T(1024)S(1)} %reshape.405, f32[224,1536]{1,0:T(8,128)} %fusion.70, bf16[224,4096]{1,0:T(8,128)(2,1)S(1)} %get-tuple-element.79.refs_9_, ...), kind=kOutput, calls=%fused_computation.50 | convolution fusion | flops 2820978944 | bytes 18557696 | tf_op jit(solution)/shard_map/dot_general | solution.py:471
  270.1 2.4 convolution_convert_fusion
  272.4 4.7 reshape.418
  277.2 3.6 copy.77
  280.8 2.8 fusion.27
  283.6 2.0 copy.84
  285.6 2.2 convert_element_type.216
  287.8 2.5 fusion.3
  292.0 1.5 copy.81
  293.5 2.5 reshape.394
  296.0 1.2 multiply_subtract_fusion.1
  298.0 1.9 copy.85
  299.9 2.1 pad_maximum_fusion.2.refs_6_
  302.0 1.4 multiply_bitcast_fusion
  303.4 2.4 copy.79
  305.7 3.1 reshape.393
  308.9 1.6 multiply_subtract_fusion
  310.7 4.3 fusion.71
  318.6 1.9 fusion.18
  320.5 2.3 copy.87.refs_5_
  324.8 218.3 %exchange_rows.1 = (bf16[2,224,1536]{2,1,0:T(8,128)(2,1)}, bf16[2,224,1536]{2,1,0:T(8,128)(2,1)}, bf16[2,224,1536]{2,1,0:T(8,128)(2,1)}, bf16[2,224,4096]{2,1,0:...) custom-call(bf16[224,1536]{1,0:T(8,128)(2,1)} %get-tuple-element.84., ...), custom_call_target="tpu_custom_call" | custom-call | tf_op jit(solution)/shard_map/exchange_rows/pallas_call | solution.py:249
  543.2 8.4 %bitcast_convert_fusion = bf16[4096,768]{1,0:T(8,128)(2,1)} fusion(bf16[2,224,4096]{2,1,0:T(8,128)(2,1)} %get-tuple-element.56, bf16[2,224,768]{2,1,0:T(8,128)(2,1)} %get-tuple-element.57), kind=kOutput, calls=%fused_computation.1 | convolution fusion | flops 2821718016 | bytes 10649600 | tf_op jit(solution)/shard_map/dot_general | solution.py:471
  551.6 5.4 bitcast_convert_fusion.1
  557.1 5.6 bitcast_convert_fusion.2
  562.7 2.8 bitcast_convert_fusion.3
  565.6 2.8 bitcast_convert_fusion.4
  568.4 2.9 bitcast_convert_fusion.5
  572.1 9.0 %fusion.2 = bf16[224,1536]{1,0:T(8,128)(2,1)} fusion(f32[224,1536]{1,0:T(8,128)S(1)} %get-tuple-element.110, bf16[224,4096]{1,0:T(8,128)(2,1)} %get-tuple-element.77.refs_3_, bf16[4096,1536]{1,0:T(8,128)(2,1)} %bitcast.287), kind=kOutput, calls=%fused_computation.17 | convolution fusion | flops 2819260416 | bytes 16482304 | tf_op jit(solution)/shard_map/dot_general | solution.py:471
  581.2 194.0 %reduce_grads.1 = (bf16[96,1536]{1,0:T(8,128)(2,1)}, bf16[96,1536]{1,0:T(8,128)(2,1)}, bf16[96,1536]{1,0:T(8,128)(2,1)}, bf16[96,4096]{1,0:T(8,128)(2,1)}, bf16[...) custom-call(bf16[2,4,192,768]{3,2,1,0:T(8,128)(2,1)} %bitcast.274, ...), custom_call_target="tpu_custom_call" | custom-call | tf_op jit(solution)/shard_map/reduce_grads/pallas_call | solution.py:430
  775.3 1.5 fusion.31
  777.7 1.3 convert_element_type.229
  779.0 1.3 convert_element_type.230
  780.3 1.3 convert_element_type.231
  (191 shorter events, 30.5 us)
Async XLA Ops:
  2.8 176.9 %copy-start.40 = (pred[112]{0:T(512)(128)(4,1)}, pred[112]{0:T(512)(128)(4,1)S(1)}, u32[]{:S(2)}) copy-start(pred[112]{0:T(512)(128)(4,1)S(1)} %get-tuple-element.104) | copy-start | bytes 340
  3.4 176.3 %copy-start.42 = (pred[112]{0:T(512)(128)(4,1)}, pred[112]{0:T(512)(128)(4,1)S(1)}, u32[]{:S(2)}) copy-start(pred[112]{0:T(512)(128)(4,1)S(1)} %get-tuple-element.106) | copy-start | bytes 340
  4.8 174.9 %copy-start.19 = (bf16[2,64,1536]{2,1,0:T(8,128)(2,1)S(1)}, bf16[2,64,1536]{2,1,0:T(8,128)(2,1)}, u32[]{:S(2)}) copy-start(bf16[2,64,1536]{2,1,0:T(8,128)(2,1)} %refs_8_.1) | copy-start | bytes 1179652
  4.8 174.9 %copy-start.20 = (bf16[2,64,1536]{2,1,0:T(8,128)(2,1)S(1)}, bf16[2,64,1536]{2,1,0:T(8,128)(2,1)}, u32[]{:S(2)}) copy-start(bf16[2,64,1536]{2,1,0:T(8,128)(2,1)} %refs_9_.1) | copy-start | bytes 1179652
  181.2 10.5 %copy-start.29 = (bf16[2,4,2,16,256]{4,3,2,1,0:T(8,128)(2,1)S(1)}, bf16[2,4,2,16,256]{4,3,2,1,0:T(8,128)(2,1)}, u32[]{:S(2)}) copy-start(bf16[2,4,2,16,256]{4,3,2,1,0:T(8,128)(2,1)} %get-tuple-element.40) | copy-start | bytes 393220
  191.7 20.6 %copy-start.35 = (f32[224]{0:T(256)}, f32[224]{0:T(256)S(1)}, u32[]{:S(2)}) copy-start(f32[224]{0:T(256)S(1)} %add_rsqrt_fusion.1) | copy-start | bytes 2692
  204.4 11.7 %copy-start.21 = (f32[224,48]{0,1:T(8,128)}, f32[224,48]{0,1:T(8,128)S(1)}, u32[]{:S(2)}) copy-start(f32[224,48]{0,1:T(8,128)S(1)} %get-tuple-element.96) | copy-start | bytes 129028
  204.7 13.3 %copy-start.23 = (bf16[2,112,8,48]{1,3,2,0:T(8,128)(2,1)}, bf16[2,112,8,48]{1,3,2,0:T(8,128)(2,1)S(1)}, u32[]{:S(2)}) copy-start(bf16[2,112,8,48]{1,3,2,0:T(8,128)(2,1)S(1)} %copy.67) | copy-start | bytes 516100
  220.1 2.6 copy-start.33
  229.9 6.8 copy-start.10
  229.9 6.8 copy-start.54
  247.1 10.9 %copy-start.13 = (bf16[224,4096]{1,0:T(8,128)(2,1)}, bf16[224,4096]{1,0:T(8,128)(2,1)S(1)}, u32[]{:S(2)}) copy-start(bf16[224,4096]{1,0:T(8,128)(2,1)S(1)} %get-tuple-element.78.refs_8_) | copy-start | bytes 5505028
  247.1 10.9 %copy-start.14 = (bf16[224,4096]{1,0:T(8,128)(2,1)}, bf16[224,4096]{1,0:T(8,128)(2,1)S(1)}, u32[]{:S(2)}) copy-start(bf16[224,4096]{1,0:T(8,128)(2,1)S(1)} %get-tuple-element.79.refs_9_) | copy-start | bytes 5505028
  247.1 10.9 %copy-start.31 = (f32[224]{0:T(256)S(1)}, f32[224]{0:T(256)}, u32[]{:S(2)}) copy-start(f32[224]{0:T(256)} %add_rsqrt_fusion) | copy-start | bytes 2692
  247.1 22.9 %slice-start = ((s8[4718592]{0:T(1024)(128)(4,1)}), s8[4194304]{0:T(1024)(128)(4,1)S(1)}, s32[]{:S(2)}) async-start(s8[4718592]{0:T(1024)(128)(4,1)} %bitcast.250), calls=%async_computation | async-start | bytes 8388608
  258.0 12.0 %slice-start.1 = ((s8[4718592]{0:T(1024)(128)(4,1)}), s8[524288]{0:T(1024)(128)(4,1)S(1)}, s32[]{:S(2)}) async-start(s8[4718592]{0:T(1024)(128)(4,1)} %bitcast.250), calls=%async_computation.1 | async-start | bytes 1048576
  287.7 2.5 copy-start.16
  287.7 2.5 copy-start.34
  290.3 1.4 copy-start.18
  299.9 2.1 copy-start.2
  310.7 4.3 copy-start.7
  310.7 4.3 copy-start
  310.7 4.3 copy-start.6
  315.0 1.8 copy-start.12
  315.1 1.8 copy-start.36
  316.8 1.8 copy-start.5
  316.8 1.8 copy-start.32
  316.8 1.8 copy-start.38
  543.2 8.5 %copy-start.47 = (bf16[2,224,2048]{2,1,0:T(8,128)(2,1)S(1)}, bf16[2,224,2048]{2,1,0:T(8,128)(2,1)}, u32[]{:S(2)}) copy-start(bf16[2,224,2048]{2,1,0:T(8,128)(2,1)} %get-tuple-element.55) | copy-start | bytes 5505028
  543.2 8.5 %copy-start.50 = (bf16[2,224,1536]{2,1,0:T(8,128)(2,1)S(1)}, bf16[2,224,1536]{2,1,0:T(8,128)(2,1)}, u32[]{:S(2)}) copy-start(bf16[2,224,1536]{2,1,0:T(8,128)(2,1)} %get-tuple-element.53) | copy-start | bytes 4128772
  551.6 5.4 copy-start.46
  557.1 5.6 copy-start.49
  557.1 5.6 copy-start.53
  562.7 2.9 copy-start.48
  562.7 2.9 copy-start.52
  565.6 2.8 copy-start.51
  568.4 2.9 copy-start.30
  581.1 194.0 %copy-start.43 = (pred[112]{0:T(512)(128)(4,1)S(1)}, pred[112]{0:T(512)(128)(4,1)}, u32[]{:S(2)}) copy-start(pred[112]{0:T(512)(128)(4,1)} %copy-done.42) | copy-start | bytes 340
  581.1 194.1 %copy-start.41 = (pred[112]{0:T(512)(128)(4,1)S(1)}, pred[112]{0:T(512)(128)(4,1)}, u32[]{:S(2)}) copy-start(pred[112]{0:T(512)(128)(4,1)} %copy-done.40) | copy-start | bytes 340
  581.1 194.1 %copy-start.45 = (pred[112]{0:T(512)(128)(4,1)S(1)}, pred[112]{0:T(512)(128)(4,1)}, u32[]{:S(2)}) copy-start(pred[112]{0:T(512)(128)(4,1)} %get-tuple-element.105) | copy-start | bytes 340
  581.1 194.1 %copy-start.44 = (pred[112]{0:T(512)(128)(4,1)S(1)}, pred[112]{0:T(512)(128)(4,1)}, u32[]{:S(2)}) copy-start(pred[112]{0:T(512)(128)(4,1)} %get-tuple-element.103) | copy-start | bytes 340
  581.1 194.1 %copy-start.3 = (bf16[224,1536]{1,0:T(8,128)(2,1)S(1)}, bf16[224,1536]{1,0:T(8,128)(2,1)}, u32[]{:S(2)}) copy-start(bf16[224,1536]{1,0:T(8,128)(2,1)} %get-tuple-element.85) | copy-start | bytes 2064388
  581.2 194.1 %copy-start.11 = (bf16[224,1536]{1,0:T(8,128)(2,1)S(1)}, bf16[224,1536]{1,0:T(8,128)(2,1)}, u32[]{:S(2)}) copy-start(bf16[224,1536]{1,0:T(8,128)(2,1)} %fusion.2) | copy-start | bytes 2064388
  775.3 2.4 copy-start.26
  779.0 1.3 copy-start.24
  780.3 1.3 copy-start.22
  780.3 2.2 copy-start.28
  781.6 1.7 copy-start.27
  (9 other events, 9.1 us)
